TPU v7x, 32 devices: a whole 2x2x4 slice. The times are simulated.
32 devices in a mesh: br: 4 (over y, x), bus: 8 (over z, core).
Axes of the slice: x: 2, y: 2, z: 4, core: 2. Of those that a mesh axis runs over, the one named last changes fastest.
Arguments:
- ptdf: bfloat16 [8192, 65536], P('br', 'bus'), may hold values from -0.0234375 to 0.0234375
- load_codes: int32 [65536, 1024], P('bus'), may hold values from -4096 to 4096
- limit_codes: int32 [8192], P('br'), may hold values from 64 to 320
Outputs:
- penalty: float32 [8192, 1024], P(('br', 'bus'))
- sensitivity: float32 [65536, 1024], P('bus', 'br')
All inputs are finite; a program needn't handle non-finite values.
Results may differ from a plain program's by a relative error of at most 0.004.
Values may be sent and summed in bfloat16 or wider, within the bound.
No kernel may reach another device: no remote copies, remote signals or barrier semaphores. Data moves between devices by JAX's collectives and lax.ppermute only.
A program may use at most 192 MiB of HBM per device.

v0:
```python
import jax
import jax.numpy as jnp
from jax import lax
from jax.sharding import PartitionSpec as P


def overload(flows, limit_codes):
    limits = (limit_codes.astype(jnp.float32) / 64.0)[:, None]
    magnitude = jnp.sqrt(flows * flows + 1.0)
    zvalue = 4.0 * (magnitude / limits - 1.0)
    penalty = jax.nn.softplus(zvalue) / 4.0
    adjoint = (jax.nn.sigmoid(zvalue) * flows / (magnitude * limits)).astype(jnp.bfloat16)
    return (penalty, adjoint)


def local(ptdf, load_codes, limit_codes):
    injections = (load_codes.astype(jnp.float32) / 1024.0).astype(jnp.bfloat16)
    branch_local = ptdf.shape[0]
    owned = branch_local // lax.axis_size("bus")
    offset = lax.axis_index("bus") * owned
    partial_flows = jnp.dot(ptdf, injections, preferred_element_type=jnp.float32)
    flows = lax.psum(partial_flows, "bus")
    penalty_all, adjoint_block = overload(flows, limit_codes)
    penalty = lax.dynamic_slice_in_dim(penalty_all, offset, owned, 0)
    partial_sens = lax.dot_general(
        ptdf, adjoint_block, (((0,), (0,)), ((), ())), preferred_element_type=jnp.float32
    )
    sensitivity = lax.psum_scatter(partial_sens, "br", scatter_dimension=1, tiled=True)
    return (penalty, sensitivity)


def solution(mesh):
    return jax.shard_map(
        local,
        mesh=mesh,
        in_specs=(P("br", "bus"), P("bus", None), P("br")),
        out_specs=(P(("br", "bus"), None), P("bus", "br")),
        check_vma=False,
    )
```

profile of v0, /device:TPU:0, one launch (start us, length us, event | category | flops | bytes accessed | tf_op | source)
XLA Modules:
  0.0 595.7 jit_solution(10531165951058272835)
XLA Ops:
  7.2 0.0 all-reduce.2.cloned.1.call-start
  7.2 43.6 %fusion.2 = f32[2048,1024]{0,1:T(8,128)} fusion(bf16[2048,8192]{1,0:T(8,128)(2,1)} %param.3, s32[8192,1024]{1,0:T(8,128)} %param.4), kind=kOutput, calls=%fused_computation.7 | convolution fusion | flops 34384904192 | bytes 75497472 | tf_op jit(solution)/shard_map/dot_general | solution.py:21
  50.8 0.0 copy-start
  50.8 0.0 all-reduce.2.cloned.1.call-update
  50.9 0.2 reduce-scatter.2.cloned.1.call-start
  51.1 0.4 copy-done
  51.5 177.7 %all-reduce.2.cloned.1.call-done = f32[2048,1024]{0,1:T(8,128)} async-done(((f32[2048,1024]{0,1:T(8,128)}), f32[2048,1024]{0,1:T(8,128)}) %all-reduce.2.cloned.1.call-update) | async-done | bytes 8388624 | tf_op jit(solution)/shard_map/psum | solution.py:22
  229.3 61.7 %convolution_bitcast_fusion = f32[8192,1024]{0,1:T(8,128)} fusion(bf16[2048,8192]{1,0:T(8,128)(2,1)} %param.3, f32[2048,1024]{0,1:T(8,128)} %all-reduce.2.cloned.1.call-done, f32[2048]{0:T(1024)S(1)} %convert_multiply_fusion), kind=kOutput, calls=%fused_computation.1 | convolution fusion | flops 34384904192 | bytes 75505664 | tf_op jit(solution)/shard_map/dot_general | solution.py:25
  291.0 0.0 reduce-scatter.2.cloned.1.call-update
  291.0 5.7 add_multiply_fusion
  296.8 0.6 fusion.5
  297.3 1.3 copy.5
  298.6 281.3 %reduce-scatter.2.cloned.1.call-done = f32[8192,256]{0,1:T(8,128)} async-done(((f32[8192,1024]{0,1:T(8,128)}), f32[8192,256]{0,1:T(8,128)}) %reduce-scatter.2.cloned.1.call-update) | async-done | bytes 8388624 | tf_op jit(solution)/shard_map/reduce_scatter | solution.py:28
  579.9 9.0 %copy.6 = f32[8192,256]{1,0:T(8,128)} copy(f32[8192,256]{0,1:T(8,128)} %reduce-scatter.2.cloned.1.call-done) | data formatting | bytes 16777216
  (1 shorter events, 0.0 us)
Async XLA Ops:
  7.2 222.1 %all-reduce.2.cloned.1.call-start = ((), (), s32[]{:S(2)}) async-start(), calls=%async_computation.1 | async-start | bytes 16777216 | tf_op jit(solution)/shard_map/psum | solution.py:22
  50.8 0.7 copy-start
  50.9 529.0 %reduce-scatter.2.cloned.1.call-start = ((), (), s32[]{:S(2)}) async-start(), calls=%async_computation.2 | async-start | bytes 41943040 | tf_op jit(solution)/shard_map/reduce_scatter | solution.py:28
Sparse Core Ops, SparseCore 0:
  51.0 178.2 all-reduce.1
  291.1 288.7 reduce-scatter.1
where the time goes:
time: 596 us
  waiting for transfers between devices  459 us (77%)
  matrix products  105 us (18%)
  between operations  14.1 us (2%)
  local copies, waits for them, and re-layouts  10.7 us (2%)
  other arithmetic  6.31 us (1%)
    reduce_scatter x1, waiting for transfers between devices, local(): lax.psum_scatter(partial_sens, 'br', scatter_dimension=1, tiled=True)  281 us
    psum x1, waiting for transfers between devices, local(): flows = lax.psum(partial_flows, 'bus')  178 us
    dot_general x1, matrix products, local(): lax.dot_general(ptdf, adjoint_block, (((0,), (0,)), ((), ())), preferred_...  61.7 us
    dot_general x1, matrix products, local(): jnp.dot(ptdf, injections, preferred_element_type=jnp.float32)  43.6 us
  transfers between devices with their start and end apart: 2, of which 2 were waited for; matrix products, arithmetic and copies ran while one was open for 1% of the time, Pallas kernels for 0%

commit v1 on v0

v1 whole, which is shorter than its diff:
```python
import functools

import jax
import jax.numpy as jnp
from jax import lax
from jax.experimental import pallas as pl
from jax.experimental.pallas import tpu as pltpu
from jax.sharding import PartitionSpec as P

MIB = 2**20
VMEM = 56 * MIB


def params():
    return pltpu.CompilerParams(vmem_limit_bytes=VMEM)


def cost(flops, nbytes, trans=0):
    return pl.CostEstimate(flops=int(flops), bytes_accessed=int(nbytes), transcendentals=int(trans))


def penalty_and_adjoint(flows, limits):
    magnitude = jnp.sqrt(flows * flows + 1.0)
    zvalue = 4.0 * (magnitude / limits - 1.0)
    penalty = (jnp.maximum(zvalue, 0.0) + jnp.log1p(jnp.exp(-jnp.abs(zvalue)))) * 0.25
    adjoint = (jax.nn.sigmoid(zvalue) * flows / (magnitude * limits)).astype(jnp.bfloat16)
    return penalty, adjoint


def flows_kernel(groups, chips, own, pos, ptdf, *refs):
    codes, (keep, away, total) = refs[:groups], refs[groups:]
    k = pl.program_id(0)
    wide = codes[0].shape[1]
    for g in range(groups):
        injections = (codes[g][...].astype(jnp.float32) * (1.0 / 1024.0)).astype(jnp.bfloat16)
        part = jnp.dot(ptdf[...], injections, preferred_element_type=jnp.float32)
        cols = slice(g * wide, (g + 1) * wide)

        @pl.when(k == 0)
        def _():
            total[:, cols] = part

        @pl.when(k > 0)
        def _():
            total[:, cols] += part

    @pl.when(k == pl.num_programs(0) - 1)
    def _():
        core = pos[1]
        for chip in range(chips):
            rows = slice(chip * own, (chip + 1) * own)
            keep[rows, :] = total[pl.ds(pl.multiple_of((2 * chip + core) * own, own), own), :]
            away[rows, :] = total[pl.ds(pl.multiple_of((2 * chip + 1 - core) * own, own), own), :]


def partial_flows(pos, ptdf, codes, first, groups, wide, chips, depth):
    rows, buses = ptdf.shape
    own = rows // (2 * chips)
    hours = groups * wide
    half = jax.ShapeDtypeStruct((rows // 2, hours), jnp.float32)
    spec = pl.BlockSpec((rows // 2, hours), lambda k, pos: (0, 0))
    return pl.pallas_call(
        functools.partial(flows_kernel, groups, chips, own),
        out_shape=(half, half),
        grid_spec=pltpu.PrefetchScalarGridSpec(
            num_scalar_prefetch=1,
            grid=(buses // depth,),
            in_specs=[pl.BlockSpec((rows, depth), lambda k, pos: (0, k))]
            + [pl.BlockSpec((depth, wide), lambda k, pos, g=g: (k, pos[first + g])) for g in range(groups)],
            out_specs=(spec, spec),
            scratch_shapes=[pltpu.VMEM((rows, hours), jnp.float32)],
        ),
        compiler_params=params(),
        cost_estimate=cost(2 * rows * buses * hours, 2 * rows * buses + 4 * buses * hours),
        name="flows",
    )(pos, ptdf, *[codes] * groups)


def pair_kernel(chips, pos, keep, came, mine, *sends):
    chip, own = pos[0], mine.shape[0]
    for k in range(chips):
        rows = pl.ds(pl.multiple_of(lax.rem(chip + k, chips) * own, own), own)
        both = keep[rows, :] + came[rows, :]
        if k == 0:
            mine[...] = both
        else:
            sends[k - 1][...] = both.astype(jnp.bfloat16)


def pair_sum(pos, keep, came, chips):
    rows, hours = keep.shape
    own = rows // chips
    vmem = pl.BlockSpec(memory_space=pltpu.VMEM)
    return pl.pallas_call(
        functools.partial(pair_kernel, chips),
        out_shape=[jax.ShapeDtypeStruct((own, hours), jnp.float32)]
        + [jax.ShapeDtypeStruct((own, hours), jnp.bfloat16)] * (chips - 1),
        in_specs=[pl.BlockSpec(memory_space=pltpu.SMEM), vmem, vmem],
        out_specs=[vmem] * chips,
        compiler_params=params(),
        cost_estimate=cost(rows * hours, 10 * rows * hours),
        name="pair_sum",
    )(pos, keep, came)


def overload_kernel(others, pos, limits, mine, *refs):
    came, (penalty, adjoint) = refs[:others], refs[-2:]
    flows = mine[...]
    for part in came:
        flows += part[...].astype(jnp.float32)
    penalty[...], adjoint[...] = penalty_and_adjoint(flows, limits[...])


def overload(pos, limits, mine, came, penalty, hours_all, first, groups, wide):
    own = mine.shape[0]
    block = pl.BlockSpec((own, wide), lambda g, pos: (0, g))
    place = pl.BlockSpec((own, wide), lambda g, pos: (0, pos[first + g]))
    operands = [pos, limits, mine, *came]
    in_specs = [pl.BlockSpec((own, 1), lambda g, pos: (0, 0))] + [block] * (1 + len(came))
    aliases = {}
    if penalty is not None:
        aliases = {len(operands): 0}
        operands.append(penalty)
        in_specs.append(pl.BlockSpec(memory_space=pl.ANY))
    return pl.pallas_call(
        functools.partial(overload_kernel, len(came)),
        out_shape=(
            jax.ShapeDtypeStruct((own, hours_all), jnp.float32),
            jax.ShapeDtypeStruct(mine.shape, jnp.bfloat16),
        ),
        grid_spec=pltpu.PrefetchScalarGridSpec(
            num_scalar_prefetch=1, grid=(groups,), in_specs=in_specs, out_specs=(place, block)
        ),
        input_output_aliases=aliases,
        compiler_params=params(),
        cost_estimate=cost(20 * mine.size, 16 * mine.size, 4 * mine.size),
        name="overload",
    )(*operands)


def sens_kernel(chips, own, adds, final, pos, ptdf, *refs):
    mine, swapped = refs[:chips], refs[chips : 2 * chips]
    extra, (out, adjoint) = refs[2 * chips : 2 * chips + adds], refs[-2:]

    @pl.when(pl.program_id(0) == 0)
    def _():
        chip, core = pos[0], pos[1]
        for k in range(chips):
            slot = 2 * lax.rem(chip + chips - k, chips)
            adjoint[pl.ds(pl.multiple_of((slot + core) * own, own), own), :] = mine[k][...]
            adjoint[pl.ds(pl.multiple_of((slot + 1 - core) * own, own), own), :] = swapped[k][...]

    part = lax.dot_general(
        ptdf[...], adjoint[...], (((0,), (0,)), ((), ())), preferred_element_type=jnp.float32
    )
    for other in extra:
        part += other[...].astype(jnp.float32)
    out[...] = part.astype(out.dtype)


def partial_sens(pos, ptdf, mine, swapped, column, wide, half, block, adds=(), into=None, final=False):
    chips = len(mine)
    rows, buses = ptdf.shape
    own = rows // (2 * chips)
    steps = buses // 2 // block
    place = pl.BlockSpec((block, wide), lambda i, pos: (half * steps + i, 0))
    local = pl.BlockSpec((block, wide), lambda i, pos: (i, 0))
    operands = [pos, ptdf, *mine, *swapped, *adds]
    in_specs = (
        [pl.BlockSpec((rows, block), lambda i, pos: (0, half * steps + i))]
        + [pl.BlockSpec((own, wide), lambda i, pos: (0, column))] * (2 * chips)
        + [local] * len(adds)
    )
    aliases = {}
    if into is not None:
        aliases = {len(operands): 0}
        operands.append(into)
        in_specs.append(pl.BlockSpec(memory_space=pl.ANY))
    return pl.pallas_call(
        functools.partial(sens_kernel, chips, own, len(adds), final),
        out_shape=jax.ShapeDtypeStruct((buses, wide), jnp.float32)
        if final
        else jax.ShapeDtypeStruct((buses // 2, wide), jnp.bfloat16),
        grid_spec=pltpu.PrefetchScalarGridSpec(
            num_scalar_prefetch=1,
            grid=(steps,),
            in_specs=in_specs,
            out_specs=place if final else local,
            scratch_shapes=[pltpu.VMEM((rows, wide), jnp.bfloat16)],
        ),
        input_output_aliases=aliases,
        compiler_params=params(),
        cost_estimate=cost(rows * buses * wide, rows * buses + buses * wide),
        name="sens",
    )(*operands)


def add_kernel(total, came, out):
    out[...] = total[...] + came[...].astype(jnp.float32)


def add_into(total, came, half, block):
    rows, wide = came.shape
    steps = rows // block
    place = pl.BlockSpec((block, wide), lambda i: (half * steps + i, 0))
    return pl.pallas_call(
        add_kernel,
        out_shape=jax.ShapeDtypeStruct(total.shape, total.dtype),
        grid=(steps,),
        in_specs=[place, pl.BlockSpec((block, wide), lambda i: (i, 0))],
        out_specs=place,
        input_output_aliases={0: 0},
        compiler_params=params(),
        cost_estimate=cost(came.size, 10 * came.size),
        name="add_last",
    )(total, came)


def local_tree(ptdf, load_codes, limit_codes):
    cores = lax.axis_size("bus")
    chips = cores // 2
    rows, buses = ptdf.shape
    hours_all = load_codes.shape[1]
    own = rows // cores
    wide = hours_all // 4
    me, spot = lax.axis_index("br"), lax.axis_index("bus")
    far, over, up, home = me ^ 3, me ^ 1, me ^ 2, me
    pos = jnp.stack([spot // 2, spot % 2, far, over, up, home]).astype(jnp.int32)
    limits = lax.dynamic_slice_in_dim(limit_codes, spot * own, own, 0).astype(jnp.float32)[:, None] / 64.0
    depth = min(1024, buses)
    block = min(1024, buses // 2)

    def across(x, bit):
        return lax.ppermute(x, "br", [(i, i ^ bit) for i in range(4)])

    def swap(x):
        return lax.ppermute(x, "bus", [(i, i ^ 1) for i in range(cores)])

    def along(x, k):
        return lax.ppermute(x, "bus", [(i, (i + 2 * k) % cores) for i in range(cores)])

    def adjoints(first, groups, penalty):
        keep, away = partial_flows(pos, ptdf, load_codes, first, groups, wide, chips, depth)
        mine, *sends = pair_sum(pos, keep, swap(away), chips)
        came = [along(sends[k - 1], k) for k in range(1, chips)]
        penalty, adjoint = overload(pos, limits, mine, came, penalty, hours_all, first, groups, wide)
        held = [adjoint] + [along(adjoint, k) for k in range(1, chips)]
        return penalty, (held, [swap(x) for x in held])

    def sens(adjoint, column, half, **more):
        return partial_sens(pos, ptdf, *adjoint, column, wide, half, block, **more)

    penalty, adj_far = adjoints(2, 1, None)
    far_a = across(sens(adj_far, 0, 0), 1)
    far_b = across(sens(adj_far, 0, 1), 2)
    penalty, adj_mid = adjoints(3, 2, penalty)
    over_a = across(sens(adj_mid, 0, 0), 1)
    up_b = across(sens(adj_mid, 1, 1), 2)
    penalty, adj_home = adjoints(5, 1, penalty)
    up_a = across(sens(adj_mid, 1, 0, adds=(far_a,)), 2)
    over_b = across(sens(adj_mid, 0, 1, adds=(far_b,)), 1)
    total = sens(adj_home, 0, 0, adds=(over_a,), final=True)
    total = sens(adj_home, 0, 1, adds=(up_b,), final=True, into=total)
    total = add_into(total, up_a, 0, block)
    total = add_into(total, over_b, 1, block)
    return penalty, total


def local_general(ptdf, load_codes, limit_codes):
    own = ptdf.shape[0] // lax.axis_size("bus")
    injections = (load_codes.astype(jnp.float32) / 1024.0).astype(jnp.bfloat16)
    partial_flow = jnp.dot(ptdf, injections, preferred_element_type=jnp.float32)
    flows = lax.psum_scatter(partial_flow, "bus", scatter_dimension=0, tiled=True)
    codes = lax.dynamic_slice_in_dim(limit_codes, lax.axis_index("bus") * own, own, 0)
    penalty, mine = penalty_and_adjoint(flows, codes.astype(jnp.float32)[:, None] / 64.0)
    adjoint = lax.all_gather(mine, "bus", axis=0, tiled=True)
    part = lax.dot_general(
        ptdf, adjoint, (((0,), (0,)), ((), ())), preferred_element_type=jnp.float32
    )
    return penalty, lax.psum_scatter(part, "br", scatter_dimension=1, tiled=True)


def solution(mesh):
    tree = mesh.shape["br"] == 4 and mesh.shape["bus"] % 2 == 0
    return jax.shard_map(
        local_tree if tree else local_general,
        mesh=mesh,
        in_specs=(P("br", "bus"), P("bus", None), P("br")),
        out_specs=(P(("br", "bus"), None), P("bus", "br")),
        check_vma=False,
    )
```

time: 596 us -> 335 us (0.56)
  waiting for transfers between devices: 459 us -> 63.9 us
  Pallas kernels: 0 us -> 203 us
  matrix products: 105 us -> 0 us
  starting transfers between devices: 0.26 us -> 52.1 us
  between operations: 14.1 us -> 0.9 us
    reduce_scatter x1 -> x0, waiting for transfers between devices: 281 us -> none  [local(): lax.psum_scatter(partial_sens, 'br', scatter_dimension=1, tiled=True)]
    pallas_call x0 -> x19, Pallas kernels: none -> 203 us  [the longest x8 88.7 us: partial_sens(): pl.pallas_call(functools.partial(sens_kernel, chips, own, len(adds), fina...]
    psum x1 -> x0, waiting for transfers between devices: 178 us -> none  [local(): flows = lax.psum(partial_flows, 'bus')]
    dot_general x2 -> x0, matrix products: 105 us -> none  [the longest x1 61.7 us: local(): lax.dot_general(ptdf, adjoint_block, (((0,), (0,)), ((), ())), preferred_...]
    ppermute x0 -> x39, waiting for transfers between devices: none -> 63.9 us  [the longest x18 58.7 us: along(): lax.ppermute(x, 'bus', [(i, (i + 2 * k) % cores) for i in range(cores)])]
    ppermute x0 -> x39, starting transfers between devices: none -> 52.1 us  [the longest x18 42.8 us: along(): lax.ppermute(x, 'bus', [(i, (i + 2 * k) % cores) for i in range(cores)])]
  transfers between devices with their start and end apart: 2 -> 39, of which waited for: 2 -> 17; matrix products, arithmetic and copies ran while one was open for 1% -> 0% of each run, Pallas kernels for 0% -> 53%
where the time goes in v1:
time: 335 us; the launch traced here: 334 us
  Pallas kernels  203 us (61%)
  waiting for transfers between devices  63.9 us (19%)
  starting transfers between devices  52.1 us (16%)
  local copies, waits for them, and re-layouts  13.2 us (4%)
    pallas_call x8, Pallas kernels, partial_sens(): pl.pallas_call(functools.partial(sens_kernel, chips, own, len(adds), fina...  88.7 us
    pallas_call x3, Pallas kernels, partial_flows(): pl.pallas_call(functools.partial(flows_kernel, groups, chips, own), out_s...  86.6 us
    ppermute x18, waiting for transfers between devices, along(): lax.ppermute(x, 'bus', [(i, (i + 2 * k) % cores) for i in range(cores)])  58.7 us
    ppermute x18, starting transfers between devices, along(): lax.ppermute(x, 'bus', [(i, (i + 2 * k) % cores) for i in range(cores)])  42.8 us
    unnamed x76, local copies, waits for them, and re-layouts  11.8 us
    pallas_call x2, Pallas kernels, add_into(): pl.pallas_call(add_kernel, out_shape=jax.ShapeDtypeStruct(total.shape, to...  10.2 us
    pallas_call x3, Pallas kernels, overload(): pl.pallas_call(functools.partial(overload_kernel, len(came)), out_shape=(...  9.4 us
    pallas_call x3, Pallas kernels, pair_sum(): pl.pallas_call(functools.partial(pair_kernel, chips), out_shape=[jax.Shap...  8.5 us
  transfers between devices with their start and end apart: 39, of which 17 were waited for; matrix products, arithmetic and copies ran while one was open for 0% of the time, Pallas kernels for 53%

profile of v1, /device:TPU:0, one launch (start us, length us, event | category | flops | bytes accessed | tf_op | source)
XLA Modules:
  0.0 334.4 jit_solution(3329183215749824165)
XLA Ops:
  0.7 0.7 stack.27.pos
  1.3 20.0 %flows.5 = (f32[1024,256]{1,0:T(8,128)}, f32[1024,256]{1,0:T(8,128)}) custom-call(s32[6]{0:T(128)} %stack.27.pos, bf16[2048,8192]{1,0:T(8,128)(2,1)} %ptdf.21, s32[8192,1024]{1,0:T(8,128)} %refs_0_.5), custom_call_target="tpu_custom_call" | custom-call | flops 8589934592 | bytes 41943040 | tf_op jit(solution)/shard_map/flows/pallas_call | solution.py:62
  21.8 46.6 %flows.4 = (f32[1024,512]{1,0:T(8,128)}, f32[1024,512]{1,0:T(8,128)}) custom-call(s32[6]{0:T(128)} %stack.27.pos, bf16[2048,8192]{1,0:T(8,128)(2,1)} %ptdf.21, s32[8192,1024]{1,0:T(8,128)} %refs_0_.5, s32[8192,1024]{1,0:T(8,128)} %refs_0_.5), custom_call_target="tpu_custom_call" | custom-call | flops 17179869184 | bytes 50331648 | tf_op jit(solution)/shard_map/flows/pallas_call | solution.py:62
  68.4 1.0 copy-done.12
  69.4 2.5 pair_sum.5
  71.9 3.0 collective-permute-start.9
  74.9 2.6 collective-permute-start.10
  77.5 1.4 collective-permute-start.11
  78.8 0.8 convert_multiply_fusion
  79.6 0.8 copy.12.limits
  80.4 1.1 collective-permute-done.9.refs_0_
  81.5 5.0 %collective-permute-done.10.refs_1_ = bf16[256,256]{1,0:T(8,128)(2,1)S(1)} collective-permute-done((bf16[256,256]{1,0:T(8,128)(2,1)}, bf16[256,256]{1,0:T(8,128)(2,1)S(1)}, u32[]{:S(2)}, u32[]{:S(2)}) %collective-permute-start.10) | collective-permute-done | bytes 131104 | tf_op jit(solution)/shard_map/ppermute | solution.py:240
  87.2 2.9 overload.3
  90.2 3.2 collective-permute-start.28
  93.4 1.7 collective-permute-start.29
  95.1 0.7 collective-permute-start.30
  95.8 3.1 collective-permute-done.28.refs_1_
  98.9 4.5 %collective-permute-done.29.refs_2_ = bf16[256,256]{1,0:T(8,128)(2,1)S(1)} collective-permute-done((bf16[256,256]{1,0:T(8,128)(2,1)}, bf16[256,256]{1,0:T(8,128)(2,1)S(1)}, u32[]{:S(2)}, u32[]{:S(2)}) %collective-permute-start.29) | collective-permute-done | bytes 131104 | tf_op jit(solution)/shard_map/ppermute | solution.py:240
  103.9 20.1 %flows.3 = (f32[1024,256]{1,0:T(8,128)}, f32[1024,256]{1,0:T(8,128)}) custom-call(s32[6]{0:T(128)} %stack.27.pos, bf16[2048,8192]{1,0:T(8,128)(2,1)} %ptdf.21, s32[8192,1024]{1,0:T(8,128)} %refs_0_.5), custom_call_target="tpu_custom_call" | custom-call | flops 8589934592 | bytes 41943040 | tf_op jit(solution)/shard_map/flows/pallas_call | solution.py:62
  125.5 10.8 %sens.12 = bf16[4096,256]{1,0:T(8,128)(2,1)} custom-call(s32[6]{0:T(128)} %stack.27.pos, bf16[2048,8192]{1,0:T(8,128)(2,1)} %ptdf.21, bf16[256,256]{1,0:T(8,128)(2,1)} %get-tuple-element.49.refs_0_, bf16[256,256]{1,0:T(8,128)(2,1)} %copy-done.13, bf16[256,256]{1,0:T(8,128)(2,1)} %copy-done.14, bf16[256,256]{1,0:T(8,128)(2,1)} %copy-done.15, ...), custom_call_target="tpu_custom_call" | custom-call | flops 4294967296 | bytes 18874368 | tf_op jit(solution)/shard_map/sens/pallas_call | solution.py:179
  136.3 1.5 collective-permute-start.35
  137.8 1.3 copy-done.10
  139.2 3.5 %pair_sum.4 = (f32[256,512]{1,0:T(8,128)}, bf16[256,512]{1,0:T(8,128)(2,1)}, bf16[256,512]{1,0:T(8,128)(2,1)}, bf16[256,512]{1,0:T(8,128)(2,1)}) custom-call(s32[6]{0:T(128)} %stack.27.pos, f32[1024,512]{1,0:T(8,128)} %get-tuple-element.32.keep, f32[1024,512]{1,0:T(8,128)} %copy-done.10), custom_call_target="tpu_custom_call" | custom-call | flops 524288 | bytes 5242880 | tf_op jit(solution)/shard_map/pair_sum/pallas_call | solution.py:94
  142.7 3.2 collective-permute-start.5
  145.9 2.1 collective-permute-start.6
  148.2 10.8 %sens.14 = bf16[4096,256]{1,0:T(8,128)(2,1)} custom-call(s32[6]{0:T(128)} %stack.27.pos, bf16[2048,8192]{1,0:T(8,128)(2,1)} %ptdf.21, bf16[256,256]{1,0:T(8,128)(2,1)} %get-tuple-element.49.refs_0_, bf16[256,256]{1,0:T(8,128)(2,1)} %copy-done.13, bf16[256,256]{1,0:T(8,128)(2,1)} %copy-done.14, bf16[256,256]{1,0:T(8,128)(2,1)} %copy-done.15, ...), custom_call_target="tpu_custom_call" | custom-call | flops 4294967296 | bytes 18874368 | tf_op jit(solution)/shard_map/sens/pallas_call | solution.py:179
  159.1 1.6 collective-permute-start.37
  160.7 4.9 %collective-permute-done.6.refs_1_ = bf16[256,512]{1,0:T(8,128)(2,1)S(1)} collective-permute-done((bf16[256,512]{1,0:T(8,128)(2,1)}, bf16[256,512]{1,0:T(8,128)(2,1)S(1)}, u32[]{:S(2)}, u32[]{:S(2)}) %collective-permute-start.6) | collective-permute-done | bytes 262176 | tf_op jit(solution)/shard_map/ppermute | solution.py:240
  165.6 0.7 copy-done.28
  166.4 3.5 %overload.4 = (f32[256,1024]{1,0:T(8,128)}, bf16[256,512]{1,0:T(8,128)(2,1)}) custom-call(s32[6]{0:T(128)} %stack.27.pos, f32[256,1]{1,0:T(8,128)} %copy.12.limits, f32[256,512]{1,0:T(8,128)} %get-tuple-element.34.mine, bf16[256,512]{1,0:T(8,128)(2,1)} %copy-done.27, bf16[256,512]{1,0:T(8,128)(2,1)} %copy-done.28, ...), custom_call_target="tpu_custom_call", output_to_operand_aliasing={{0}: (6, {})} | custom-call | flops 2621440 | bytes 2097152 | tf_op jit(solution)/shard_map/overload/pallas_call | solution.py:125
  169.9 6.0 %collective-permute-start.19 = (bf16[256,512]{1,0:T(8,128)(2,1)}, bf16[256,512]{1,0:T(8,128)(2,1)S(1)}, u32[]{:S(2)}, u32[]{:S(2)}) collective-permute-start(bf16[256,512]{1,0:T(8,128)(2,1)} %get-tuple-element.48.refs_0_), channel_id=1, source_target_pairs={{0,2},{1,3},{2,4},{3,5},{4,6},{5,7},{6,0},{7,1},{8,10},{9,11},{10,... | collective-permute-start | bytes 786440 | tf_op jit(solution)/shard_map/ppermute | solution.py:240
  176.4 2.0 collective-permute-start.21
  178.4 5.0 %collective-permute-done.19.refs_1_ = bf16[256,512]{1,0:T(8,128)(2,1)S(1)} collective-permute-done((bf16[256,512]{1,0:T(8,128)(2,1)}, bf16[256,512]{1,0:T(8,128)(2,1)S(1)}, u32[]{:S(2)}, u32[]{:S(2)}) %collective-permute-start.19) | collective-permute-done | bytes 262176 | tf_op jit(solution)/shard_map/ppermute | solution.py:240
  183.4 9.6 %collective-permute-done.20.refs_2_ = bf16[256,512]{1,0:T(8,128)(2,1)S(1)} collective-permute-done((bf16[256,512]{1,0:T(8,128)(2,1)}, bf16[256,512]{1,0:T(8,128)(2,1)S(1)}, u32[]{:S(2)}, u32[]{:S(2)}) %collective-permute-start.20) | collective-permute-done | bytes 262176 | tf_op jit(solution)/shard_map/ppermute | solution.py:240
  193.9 2.5 pair_sum.3
  196.4 6.0 %collective-permute-start.1 = (bf16[256,256]{1,0:T(8,128)(2,1)}, bf16[256,256]{1,0:T(8,128)(2,1)S(1)}, u32[]{:S(2)}, u32[]{:S(2)}) collective-permute-start(bf16[256,256]{1,0:T(8,128)(2,1)} %get-tuple-element.29), channel_id=1, source_target_pairs={{0,2},{1,3},{2,4},{3,5},{4,6},{5,7},{6,0},{7,1},{8,10},{9,11},{10,... | collective-permute-start | bytes 393224 | tf_op jit(solution)/shard_map/ppermute | solution.py:240
  203.1 0.7 copy-done.6
  203.8 10.8 %sens.9 = bf16[4096,256]{1,0:T(8,128)(2,1)} custom-call(s32[6]{0:T(128)} %stack.27.pos, bf16[2048,8192]{1,0:T(8,128)(2,1)} %ptdf.21, bf16[256,512]{1,0:T(8,128)(2,1)} %get-tuple-element.48.refs_0_, bf16[256,512]{1,0:T(8,128)(2,1)} %copy-done, bf16[256,512]{1,0:T(8,128)(2,1)} %copy-done.1, bf16[256,512]{1,0:T(8,128)(2,1)} %copy-done.2, ...), custom_call_target="tpu_custom_call" | custom-call | flops 4294967296 | bytes 18874368 | tf_op jit(solution)/shard_map/sens/pallas_call | solution.py:179
  215.1 10.9 %sens.8 = bf16[4096,256]{1,0:T(8,128)(2,1)} custom-call(s32[6]{0:T(128)} %stack.27.pos, bf16[2048,8192]{1,0:T(8,128)(2,1)} %ptdf.21, bf16[256,512]{1,0:T(8,128)(2,1)} %get-tuple-element.48.refs_0_, bf16[256,512]{1,0:T(8,128)(2,1)} %copy-done, bf16[256,512]{1,0:T(8,128)(2,1)} %copy-done.1, bf16[256,512]{1,0:T(8,128)(2,1)} %copy-done.2, ...), custom_call_target="tpu_custom_call" | custom-call | flops 4294967296 | bytes 18874368 | tf_op jit(solution)/shard_map/sens/pallas_call | solution.py:179
  226.0 1.5 collective-permute-start.26
  227.5 11.1 %sens.13 = bf16[4096,256]{1,0:T(8,128)(2,1)} custom-call(s32[6]{0:T(128)} %stack.27.pos, bf16[2048,8192]{1,0:T(8,128)(2,1)} %ptdf.21, bf16[256,512]{1,0:T(8,128)(2,1)} %get-tuple-element.48.refs_0_, bf16[256,512]{1,0:T(8,128)(2,1)} %copy-done, bf16[256,512]{1,0:T(8,128)(2,1)} %copy-done.1, bf16[256,512]{1,0:T(8,128)(2,1)} %copy-done.2, ...), custom_call_target="tpu_custom_call" | custom-call | flops 4294967296 | bytes 18874368 | tf_op jit(solution)/shard_map/sens/pallas_call | solution.py:179
  239.2 11.1 %sens.15 = bf16[4096,256]{1,0:T(8,128)(2,1)} custom-call(s32[6]{0:T(128)} %stack.27.pos, bf16[2048,8192]{1,0:T(8,128)(2,1)} %ptdf.21, bf16[256,512]{1,0:T(8,128)(2,1)} %get-tuple-element.48.refs_0_, bf16[256,512]{1,0:T(8,128)(2,1)} %copy-done, bf16[256,512]{1,0:T(8,128)(2,1)} %copy-done.1, bf16[256,512]{1,0:T(8,128)(2,1)} %copy-done.2, ...), custom_call_target="tpu_custom_call" | custom-call | flops 4294967296 | bytes 18874368 | tf_op jit(solution)/shard_map/sens/pallas_call | solution.py:179
  250.3 1.5 collective-permute-start.38
  251.8 3.3 collective-permute-start.2
  255.1 5.3 %collective-permute-done.2.refs_1_ = bf16[256,256]{1,0:T(8,128)(2,1)S(1)} collective-permute-done((bf16[256,256]{1,0:T(8,128)(2,1)S(1)}, bf16[256,256]{1,0:T(8,128)(2,1)S(1)}, u32[]{:S(2)}, u32[]{:S(2)}) %collective-permute-start.2) | collective-permute-done | bytes 131104 | tf_op jit(solution)/shard_map/ppermute | solution.py:240
  260.4 2.6 collective-permute-start.3
  263.1 2.8 collective-permute-done.3.refs_2_
  266.5 2.9 overload.5
  269.4 7.1 %collective-permute-done.12.refs_1_ = bf16[256,256]{1,0:T(8,128)(2,1)S(1)} collective-permute-done((bf16[256,256]{1,0:T(8,128)(2,1)}, bf16[256,256]{1,0:T(8,128)(2,1)S(1)}, u32[]{:S(2)}, u32[]{:S(2)}) %collective-permute-start.12) | collective-permute-done | bytes 131104 | tf_op jit(solution)/shard_map/ppermute | solution.py:240
  276.6 1.5 collective-permute-start.13
  278.1 7.0 %collective-permute-done.13.refs_2_ = bf16[256,256]{1,0:T(8,128)(2,1)S(1)} collective-permute-done((bf16[256,256]{1,0:T(8,128)(2,1)}, bf16[256,256]{1,0:T(8,128)(2,1)S(1)}, u32[]{:S(2)}, u32[]{:S(2)}) %collective-permute-start.13) | collective-permute-done | bytes 131104 | tf_op jit(solution)/shard_map/ppermute | solution.py:240
  285.1 2.7 collective-permute-start.14
  287.9 2.8 collective-permute-done.14.refs_3_
  290.7 1.6 collective-permute-done.15.refs_4_
  292.4 1.2 collective-permute-done.16.refs_5_
  293.8 1.2 collective-permute-done.17.refs_6_
  295.1 1.2 collective-permute-done.18.refs_7_
  297.0 1.3 copy-done.9
  298.3 11.6 %sens.10.refs_9_ = f32[8192,256]{1,0:T(8,128)} custom-call(s32[6]{0:T(128)} %stack.27.pos, bf16[2048,8192]{1,0:T(8,128)(2,1)} %ptdf.21, bf16[256,256]{1,0:T(8,128)(2,1)} %get-tuple-element.47.refs_0_, bf16[256,256]{1,0:T(8,128)(2,1)} %copy-done.19, bf16[256,256]{1,0:T(8,128)(2,1)} %copy-done.21, bf16[256,256]{1,0:T(8,128)(2,1)} %copy-done.22, ...), custom_call_target="tpu_custom_call" | custom-call | flops 4294967296 | bytes 18874368 | tf_op jit(solution)/shard_map/sens/pallas_call | solution.py:179
  309.8 1.4 copy-done.8
  311.2 11.6 %sens.11.total = f32[8192,256]{1,0:T(8,128)} custom-call(s32[6]{0:T(128)} %stack.27.pos, bf16[2048,8192]{1,0:T(8,128)(2,1)} %ptdf.21, bf16[256,256]{1,0:T(8,128)(2,1)} %get-tuple-element.47.refs_0_, bf16[256,256]{1,0:T(8,128)(2,1)} %copy-done.19, bf16[256,256]{1,0:T(8,128)(2,1)} %copy-done.21, ...), custom_call_target="tpu_custom_call", output_to_operand_aliasing={{}: (11, {})} | custom-call | flops 4294967296 | bytes 18874368 | tf_op jit(solution)/shard_map/sens/pallas_call | solution.py:179
  322.8 1.3 copy-done.7
  324.1 5.1 %add_last.2.total = f32[8192,256]{1,0:T(8,128)} custom-call(f32[8192,256]{1,0:T(8,128)} %sens.11.total, bf16[4096,256]{1,0:T(8,128)(2,1)} %copy-done.7), custom_call_target="tpu_custom_call", output_to_operand_aliasing={{}: (0, {})} | custom-call | flops 1048576 | bytes 10485760 | tf_op jit(solution)/shard_map/add_last/pallas_call | solution.py:206
  329.3 5.1 %add_last.3 = f32[8192,256]{1,0:T(8,128)} custom-call(f32[8192,256]{1,0:T(8,128)} %add_last.2.total, bf16[4096,256]{1,0:T(8,128)(2,1)} %collective-permute-done.38.came), custom_call_target="tpu_custom_call", output_to_operand_aliasing={{}: (0, {})} | custom-call | flops 1048576 | bytes 10485760 | tf_op jit(solution)/shard_map/add_last/pallas_call | solution.py:206
  (112 shorter events, 8.5 us)
Async XLA Ops:
  21.3 47.1 %collective-permute-start.8 = (f32[1024,256]{1,0:T(8,128)}, f32[1024,256]{1,0:T(8,128)S(1)}, u32[]{:S(2)}, u32[]{:S(2)}) collective-permute-start(f32[1024,256]{1,0:T(8,128)} %get-tuple-element.39), channel_id=1, source_target_pairs={{0,1},{1,0},{2,3},{3,2},{4,5},{5,4},{6,7},{7,6},{8,9},{9,8},{10,11... | collective-permute-start | bytes 3145736 | tf_op jit(solution)/shard_map/ppermute | solution.py:237
  68.3 69.5 %collective-permute-start.4 = (f32[1024,512]{1,0:T(8,128)}, f32[1024,512]{1,0:T(8,128)S(1)}, u32[]{:S(2)}, u32[]{:S(2)}) collective-permute-start(f32[1024,512]{1,0:T(8,128)} %get-tuple-element.33), channel_id=1, source_target_pairs={{0,1},{1,0},{2,3},{3,2},{4,5},{5,4},{6,7},{7,6},{8,9},{9,8},{10,11... | collective-permute-start | bytes 6291464 | tf_op jit(solution)/shard_map/ppermute | solution.py:237
  71.9 9.7 %collective-permute-start.9 = (bf16[256,256]{1,0:T(8,128)(2,1)}, bf16[256,256]{1,0:T(8,128)(2,1)S(1)}, u32[]{:S(2)}, u32[]{:S(2)}) collective-permute-start(bf16[256,256]{1,0:T(8,128)(2,1)} %get-tuple-element.41), channel_id=1, source_target_pairs={{0,2},{1,3},{2,4},{3,5},{4,6},{5,7},{6,0},{7,1},{8,10},{9,11},{10,... | collective-permute-start | bytes 393224 | tf_op jit(solution)/shard_map/ppermute | solution.py:240
  74.9 11.6 %collective-permute-start.10 = (bf16[256,256]{1,0:T(8,128)(2,1)}, bf16[256,256]{1,0:T(8,128)(2,1)S(1)}, u32[]{:S(2)}, u32[]{:S(2)}) collective-permute-start(bf16[256,256]{1,0:T(8,128)(2,1)} %get-tuple-element.42), channel_id=1, source_target_pairs={{0,4},{1,5},{2,6},{3,7},{4,0},{5,1},{6,2},{7,3},{8,12},{9,13},{10,... | collective-permute-start | bytes 393224 | tf_op jit(solution)/shard_map/ppermute | solution.py:240
  77.5 9.0 %collective-permute-start.11 = (bf16[256,256]{1,0:T(8,128)(2,1)}, bf16[256,256]{1,0:T(8,128)(2,1)S(1)}, u32[]{:S(2)}, u32[]{:S(2)}) collective-permute-start(bf16[256,256]{1,0:T(8,128)(2,1)} %get-tuple-element.43), channel_id=1, source_target_pairs={{0,6},{1,7},{2,0},{3,1},{4,2},{5,3},{6,4},{7,5},{8,14},{9,15},{10,... | collective-permute-start | bytes 393224 | tf_op jit(solution)/shard_map/ppermute | solution.py:240
  81.5 5.0 %copy-start.30 = (bf16[256,256]{1,0:T(8,128)(2,1)}, bf16[256,256]{1,0:T(8,128)(2,1)S(1)}, u32[]{:S(2)}) copy-start(bf16[256,256]{1,0:T(8,128)(2,1)S(1)} %collective-permute-done.9.refs_0_) | copy-start | bytes 393220
  90.2 8.7 %collective-permute-start.28 = (bf16[256,256]{1,0:T(8,128)(2,1)}, bf16[256,256]{1,0:T(8,128)(2,1)S(1)}, u32[]{:S(2)}, u32[]{:S(2)}) collective-permute-start(bf16[256,256]{1,0:T(8,128)(2,1)} %get-tuple-element.49.refs_0_), channel_id=1, source_target_pairs={{0,2},{1,3},{2,4},{3,5},{4,6},{5,7},{6,0},{7,1},{8,10},{9,11},{10,... | collective-permute-start | bytes 393224 | tf_op jit(solution)/shard_map/ppermute | solution.py:240
  93.4 10.0 %collective-permute-start.29 = (bf16[256,256]{1,0:T(8,128)(2,1)}, bf16[256,256]{1,0:T(8,128)(2,1)S(1)}, u32[]{:S(2)}, u32[]{:S(2)}) collective-permute-start(bf16[256,256]{1,0:T(8,128)(2,1)} %get-tuple-element.49.refs_0_), channel_id=1, source_target_pairs={{0,4},{1,5},{2,6},{3,7},{4,0},{5,1},{6,2},{7,3},{8,12},{9,13},{10,... | collective-permute-start | bytes 393224 | tf_op jit(solution)/shard_map/ppermute | solution.py:240
  95.1 8.3 %collective-permute-start.30 = (bf16[256,256]{1,0:T(8,128)(2,1)}, bf16[256,256]{1,0:T(8,128)(2,1)S(1)}, u32[]{:S(2)}, u32[]{:S(2)}) collective-permute-start(bf16[256,256]{1,0:T(8,128)(2,1)} %get-tuple-element.49.refs_0_), channel_id=1, source_target_pairs={{0,6},{1,7},{2,0},{3,1},{4,2},{5,3},{6,4},{7,5},{8,14},{9,15},{10,... | collective-permute-start | bytes 393224 | tf_op jit(solution)/shard_map/ppermute | solution.py:240
  95.7 28.2 %collective-permute-start.31 = (bf16[256,256]{1,0:T(8,128)(2,1)}, bf16[256,256]{1,0:T(8,128)(2,1)S(1)}, u32[]{:S(2)}, u32[]{:S(2)}) collective-permute-start(bf16[256,256]{1,0:T(8,128)(2,1)} %get-tuple-element.49.refs_0_), channel_id=1, source_target_pairs={{0,1},{1,0},{2,3},{3,2},{4,5},{5,4},{6,7},{7,6},{8,9},{9,8},{10,11... | collective-permute-start | bytes 393224 | tf_op jit(solution)/shard_map/ppermute | solution.py:237
  98.9 25.1 %copy-start.13 = (bf16[256,256]{1,0:T(8,128)(2,1)}, bf16[256,256]{1,0:T(8,128)(2,1)S(1)}, u32[]{:S(2)}) copy-start(bf16[256,256]{1,0:T(8,128)(2,1)S(1)} %collective-permute-done.28.refs_1_) | copy-start | bytes 393220
  98.9 25.3 %collective-permute-start.32 = (bf16[256,256]{1,0:T(8,128)(2,1)S(1)}, bf16[256,256]{1,0:T(8,128)(2,1)S(1)}, u32[]{:S(2)}, u32[]{:S(2)}) collective-permute-start(bf16[256,256]{1,0:T(8,128)(2,1)S(1)} %collective-permute-done.28.refs_1_), channel_id=1, source_target_pairs={{0,1},{1,0},{2,3},{3,2},{4,5},{5,4},{6,7},{7,6},{8,9},{9,8},{10,11... | collective-permute-start | bytes 393224 | tf_op jit(solution)/shard_map/ppermute | solution.py:237
  103.4 20.6 %copy-start.14 = (bf16[256,256]{1,0:T(8,128)(2,1)}, bf16[256,256]{1,0:T(8,128)(2,1)S(1)}, u32[]{:S(2)}) copy-start(bf16[256,256]{1,0:T(8,128)(2,1)S(1)} %collective-permute-done.29.refs_2_) | copy-start | bytes 393220
  103.4 20.8 %collective-permute-start.33 = (bf16[256,256]{1,0:T(8,128)(2,1)S(1)}, bf16[256,256]{1,0:T(8,128)(2,1)S(1)}, u32[]{:S(2)}, u32[]{:S(2)}) collective-permute-start(bf16[256,256]{1,0:T(8,128)(2,1)S(1)} %collective-permute-done.29.refs_2_), channel_id=1, source_target_pairs={{0,1},{1,0},{2,3},{3,2},{4,5},{5,4},{6,7},{7,6},{8,9},{9,8},{10,11... | collective-permute-start | bytes 393224 | tf_op jit(solution)/shard_map/ppermute | solution.py:237
  103.4 20.6 %copy-start.15 = (bf16[256,256]{1,0:T(8,128)(2,1)}, bf16[256,256]{1,0:T(8,128)(2,1)S(1)}, u32[]{:S(2)}) copy-start(bf16[256,256]{1,0:T(8,128)(2,1)S(1)} %collective-permute-done.30.refs_3_) | copy-start | bytes 393220
  103.4 20.8 %collective-permute-start.34 = (bf16[256,256]{1,0:T(8,128)(2,1)S(1)}, bf16[256,256]{1,0:T(8,128)(2,1)S(1)}, u32[]{:S(2)}, u32[]{:S(2)}) collective-permute-start(bf16[256,256]{1,0:T(8,128)(2,1)S(1)} %collective-permute-done.30.refs_3_), channel_id=1, source_target_pairs={{0,1},{1,0},{2,3},{3,2},{4,5},{5,4},{6,7},{7,6},{8,9},{9,8},{10,11... | collective-permute-start | bytes 393224 | tf_op jit(solution)/shard_map/ppermute | solution.py:237
  124.0 52.4 %collective-permute-start = (f32[1024,256]{1,0:T(8,128)}, f32[1024,256]{1,0:T(8,128)S(1)}, u32[]{:S(2)}, u32[]{:S(2)}) collective-permute-start(f32[1024,256]{1,0:T(8,128)} %get-tuple-element.27), channel_id=1, source_target_pairs={{0,1},{1,0},{2,3},{3,2},{4,5},{5,4},{6,7},{7,6},{8,9},{9,8},{10,11... | collective-permute-start | bytes 3145736 | tf_op jit(solution)/shard_map/ppermute | solution.py:237
  136.3 91.2 %collective-permute-start.35 = (bf16[4096,256]{1,0:T(8,128)(2,1)}, bf16[4096,256]{1,0:T(8,128)(2,1)}, u32[]{:S(2)}, u32[]{:S(2)}) collective-permute-start(bf16[4096,256]{1,0:T(8,128)(2,1)} %sens.12), channel_id=1, source_target_pairs={{0,8},{8,0},{16,24},{24,16},{1,9},{9,1},{17,25},{25,17},{2,10},{10... | collective-permute-start | bytes 6291464 | tf_op jit(solution)/shard_map/ppermute | solution.py:234
  137.8 1.4 copy-start.10
  142.7 16.4 %collective-permute-start.5 = (bf16[256,512]{1,0:T(8,128)(2,1)}, bf16[256,512]{1,0:T(8,128)(2,1)S(1)}, u32[]{:S(2)}, u32[]{:S(2)}) collective-permute-start(bf16[256,512]{1,0:T(8,128)(2,1)} %get-tuple-element.35), channel_id=1, source_target_pairs={{0,2},{1,3},{2,4},{3,5},{4,6},{5,7},{6,0},{7,1},{8,10},{9,11},{10,... | collective-permute-start | bytes 786440 | tf_op jit(solution)/shard_map/ppermute | solution.py:240
  145.9 19.7 %collective-permute-start.6 = (bf16[256,512]{1,0:T(8,128)(2,1)}, bf16[256,512]{1,0:T(8,128)(2,1)S(1)}, u32[]{:S(2)}, u32[]{:S(2)}) collective-permute-start(bf16[256,512]{1,0:T(8,128)(2,1)} %get-tuple-element.36), channel_id=1, source_target_pairs={{0,4},{1,5},{2,6},{3,7},{4,0},{5,1},{6,2},{7,3},{8,12},{9,13},{10,... | collective-permute-start | bytes 786440 | tf_op jit(solution)/shard_map/ppermute | solution.py:240
  147.9 17.6 %collective-permute-start.7 = (bf16[256,512]{1,0:T(8,128)(2,1)}, bf16[256,512]{1,0:T(8,128)(2,1)S(1)}, u32[]{:S(2)}, u32[]{:S(2)}) collective-permute-start(bf16[256,512]{1,0:T(8,128)(2,1)} %get-tuple-element.37), channel_id=1, source_target_pairs={{0,6},{1,7},{2,0},{3,1},{4,2},{5,3},{6,4},{7,5},{8,14},{9,15},{10,... | collective-permute-start | bytes 786440 | tf_op jit(solution)/shard_map/ppermute | solution.py:240
  159.1 6.5 %copy-start.27 = (bf16[256,512]{1,0:T(8,128)(2,1)}, bf16[256,512]{1,0:T(8,128)(2,1)S(1)}, u32[]{:S(2)}) copy-start(bf16[256,512]{1,0:T(8,128)(2,1)S(1)} %collective-permute-done.5.refs_0_) | copy-start | bytes 786436
  159.1 80.1 %collective-permute-start.37 = (bf16[4096,256]{1,0:T(8,128)(2,1)}, bf16[4096,256]{1,0:T(8,128)(2,1)}, u32[]{:S(2)}, u32[]{:S(2)}) collective-permute-start(bf16[4096,256]{1,0:T(8,128)(2,1)} %sens.14), channel_id=1, source_target_pairs={{0,16},{8,24},{16,0},{24,8},{1,17},{9,25},{17,1},{25,9},{2,18},{10... | collective-permute-start | bytes 6291464 | tf_op jit(solution)/shard_map/ppermute | solution.py:234
  169.9 13.5 %collective-permute-start.19 = (bf16[256,512]{1,0:T(8,128)(2,1)}, bf16[256,512]{1,0:T(8,128)(2,1)S(1)}, u32[]{:S(2)}, u32[]{:S(2)}) collective-permute-start(bf16[256,512]{1,0:T(8,128)(2,1)} %get-tuple-element.48.refs_0_), channel_id=1, source_target_pairs={{0,2},{1,3},{2,4},{3,5},{4,6},{5,7},{6,0},{7,1},{8,10},{9,11},{10,... | collective-permute-start | bytes 786440 | tf_op jit(solution)/shard_map/ppermute | solution.py:240
  175.9 17.1 %collective-permute-start.20 = (bf16[256,512]{1,0:T(8,128)(2,1)}, bf16[256,512]{1,0:T(8,128)(2,1)S(1)}, u32[]{:S(2)}, u32[]{:S(2)}) collective-permute-start(bf16[256,512]{1,0:T(8,128)(2,1)} %get-tuple-element.48.refs_0_), channel_id=1, source_target_pairs={{0,4},{1,5},{2,6},{3,7},{4,0},{5,1},{6,2},{7,3},{8,12},{9,13},{10,... | collective-permute-start | bytes 786440 | tf_op jit(solution)/shard_map/ppermute | solution.py:240
  176.4 17.5 %copy-start.11 = (f32[1024,256]{1,0:T(8,128)}, f32[1024,256]{1,0:T(8,128)S(1)}, u32[]{:S(2)}) copy-start(f32[1024,256]{1,0:T(8,128)S(1)} %collective-permute-done.came) | copy-start | bytes 3145732
  176.4 17.0 %collective-permute-start.21 = (bf16[256,512]{1,0:T(8,128)(2,1)}, bf16[256,512]{1,0:T(8,128)(2,1)S(1)}, u32[]{:S(2)}, u32[]{:S(2)}) collective-permute-start(bf16[256,512]{1,0:T(8,128)(2,1)} %get-tuple-element.48.refs_0_), channel_id=1, source_target_pairs={{0,6},{1,7},{2,0},{3,1},{4,2},{5,3},{6,4},{7,5},{8,14},{9,15},{10,... | collective-permute-start | bytes 786440 | tf_op jit(solution)/shard_map/ppermute | solution.py:240
  183.4 19.0 %copy-start = (bf16[256,512]{1,0:T(8,128)(2,1)}, bf16[256,512]{1,0:T(8,128)(2,1)S(1)}, u32[]{:S(2)}) copy-start(bf16[256,512]{1,0:T(8,128)(2,1)S(1)} %collective-permute-done.19.refs_1_) | copy-start | bytes 786436
  183.4 10.2 %collective-permute-start.22 = (bf16[256,512]{1,0:T(8,128)(2,1)}, bf16[256,512]{1,0:T(8,128)(2,1)S(1)}, u32[]{:S(2)}, u32[]{:S(2)}) collective-permute-start(bf16[256,512]{1,0:T(8,128)(2,1)} %get-tuple-element.48.refs_0_), channel_id=1, source_target_pairs={{0,1},{1,0},{2,3},{3,2},{4,5},{5,4},{6,7},{7,6},{8,9},{9,8},{10,11... | collective-permute-start | bytes 786440 | tf_op jit(solution)/shard_map/ppermute | solution.py:237
  193.0 9.4 %copy-start.1 = (bf16[256,512]{1,0:T(8,128)(2,1)}, bf16[256,512]{1,0:T(8,128)(2,1)S(1)}, u32[]{:S(2)}) copy-start(bf16[256,512]{1,0:T(8,128)(2,1)S(1)} %collective-permute-done.20.refs_2_) | copy-start | bytes 786436
  193.0 3.3 %collective-permute-start.23 = (bf16[256,512]{1,0:T(8,128)(2,1)S(1)}, bf16[256,512]{1,0:T(8,128)(2,1)S(1)}, u32[]{:S(2)}, u32[]{:S(2)}) collective-permute-start(bf16[256,512]{1,0:T(8,128)(2,1)S(1)} %collective-permute-done.19.refs_1_), channel_id=1, source_target_pairs={{0,1},{1,0},{2,3},{3,2},{4,5},{5,4},{6,7},{7,6},{8,9},{9,8},{10,11... | collective-permute-start | bytes 786440 | tf_op jit(solution)/shard_map/ppermute | solution.py:237
  193.4 9.1 %copy-start.2 = (bf16[256,512]{1,0:T(8,128)(2,1)}, bf16[256,512]{1,0:T(8,128)(2,1)S(1)}, u32[]{:S(2)}) copy-start(bf16[256,512]{1,0:T(8,128)(2,1)S(1)} %collective-permute-done.21.refs_3_) | copy-start | bytes 786436
  193.4 9.0 %collective-permute-start.24 = (bf16[256,512]{1,0:T(8,128)(2,1)S(1)}, bf16[256,512]{1,0:T(8,128)(2,1)S(1)}, u32[]{:S(2)}, u32[]{:S(2)}) collective-permute-start(bf16[256,512]{1,0:T(8,128)(2,1)S(1)} %collective-permute-done.20.refs_2_), channel_id=1, source_target_pairs={{0,1},{1,0},{2,3},{3,2},{4,5},{5,4},{6,7},{7,6},{8,9},{9,8},{10,11... | collective-permute-start | bytes 786440 | tf_op jit(solution)/shard_map/ppermute | solution.py:237
  193.6 8.9 %copy-start.3 = (bf16[256,512]{1,0:T(8,128)(2,1)}, bf16[256,512]{1,0:T(8,128)(2,1)S(1)}, u32[]{:S(2)}) copy-start(bf16[256,512]{1,0:T(8,128)(2,1)S(1)} %collective-permute-done.22.refs_4_) | copy-start | bytes 786436
  193.6 8.8 %collective-permute-start.25 = (bf16[256,512]{1,0:T(8,128)(2,1)S(1)}, bf16[256,512]{1,0:T(8,128)(2,1)S(1)}, u32[]{:S(2)}, u32[]{:S(2)}) collective-permute-start(bf16[256,512]{1,0:T(8,128)(2,1)S(1)} %collective-permute-done.21.refs_3_), channel_id=1, source_target_pairs={{0,1},{1,0},{2,3},{3,2},{4,5},{5,4},{6,7},{7,6},{8,9},{9,8},{10,11... | collective-permute-start | bytes 786440 | tf_op jit(solution)/shard_map/ppermute | solution.py:237
  196.4 6.1 %copy-start.4 = (bf16[256,512]{1,0:T(8,128)(2,1)}, bf16[256,512]{1,0:T(8,128)(2,1)S(1)}, u32[]{:S(2)}) copy-start(bf16[256,512]{1,0:T(8,128)(2,1)S(1)} %collective-permute-done.23.refs_5_) | copy-start | bytes 786436
  196.4 55.4 %collective-permute-start.1 = (bf16[256,256]{1,0:T(8,128)(2,1)}, bf16[256,256]{1,0:T(8,128)(2,1)S(1)}, u32[]{:S(2)}, u32[]{:S(2)}) collective-permute-start(bf16[256,256]{1,0:T(8,128)(2,1)} %get-tuple-element.29), channel_id=1, source_target_pairs={{0,2},{1,3},{2,4},{3,5},{4,6},{5,7},{6,0},{7,1},{8,10},{9,11},{10,... | collective-permute-start | bytes 393224 | tf_op jit(solution)/shard_map/ppermute | solution.py:240
  214.6 81.7 %collective-permute-start.27 = (bf16[4096,256]{1,0:T(8,128)(2,1)}, bf16[4096,256]{1,0:T(8,128)(2,1)S(1)}, u32[]{:S(2)}, u32[]{:S(2)}) collective-permute-start(bf16[4096,256]{1,0:T(8,128)(2,1)} %sens.9), channel_id=1, source_target_pairs={{0,8},{8,0},{16,24},{24,16},{1,9},{9,1},{17,25},{25,17},{2,10},{10... | collective-permute-start | bytes 6291464 | tf_op jit(solution)/shard_map/ppermute | solution.py:234
  226.0 83.8 %collective-permute-start.26 = (bf16[4096,256]{1,0:T(8,128)(2,1)}, bf16[4096,256]{1,0:T(8,128)(2,1)S(1)}, u32[]{:S(2)}, u32[]{:S(2)}) collective-permute-start(bf16[4096,256]{1,0:T(8,128)(2,1)} %sens.8), channel_id=1, source_target_pairs={{0,16},{8,24},{16,0},{24,8},{1,17},{9,25},{17,1},{25,9},{2,18},{10... | collective-permute-start | bytes 6291464 | tf_op jit(solution)/shard_map/ppermute | solution.py:234
  238.6 13.2 %copy-start.37 = (bf16[256,256]{1,0:T(8,128)(2,1)S(1)}, bf16[256,256]{1,0:T(8,128)(2,1)}, u32[]{:S(2)}) copy-start(bf16[256,256]{1,0:T(8,128)(2,1)} %get-tuple-element.30) | copy-start | bytes 393220
  238.6 21.8 %copy-start.36 = (bf16[256,256]{1,0:T(8,128)(2,1)S(1)}, bf16[256,256]{1,0:T(8,128)(2,1)}, u32[]{:S(2)}) copy-start(bf16[256,256]{1,0:T(8,128)(2,1)} %get-tuple-element.31) | copy-start | bytes 393220
  238.7 84.2 %collective-permute-start.36 = (bf16[4096,256]{1,0:T(8,128)(2,1)}, bf16[4096,256]{1,0:T(8,128)(2,1)S(1)}, u32[]{:S(2)}, u32[]{:S(2)}) collective-permute-start(bf16[4096,256]{1,0:T(8,128)(2,1)} %sens.13), channel_id=1, source_target_pairs={{0,16},{8,24},{16,0},{24,8},{1,17},{9,25},{17,1},{25,9},{2,18},{10... | collective-permute-start | bytes 6291464 | tf_op jit(solution)/shard_map/ppermute | solution.py:234
  250.3 79.0 %collective-permute-start.38 = (bf16[4096,256]{1,0:T(8,128)(2,1)}, bf16[4096,256]{1,0:T(8,128)(2,1)}, u32[]{:S(2)}, u32[]{:S(2)}) collective-permute-start(bf16[4096,256]{1,0:T(8,128)(2,1)} %sens.15), channel_id=1, source_target_pairs={{0,8},{8,0},{16,24},{24,16},{1,9},{9,1},{17,25},{25,17},{2,10},{10... | collective-permute-start | bytes 6291464 | tf_op jit(solution)/shard_map/ppermute | solution.py:234
  251.8 14.0 %copy-start.33 = (bf16[256,256]{1,0:T(8,128)(2,1)}, bf16[256,256]{1,0:T(8,128)(2,1)S(1)}, u32[]{:S(2)}) copy-start(bf16[256,256]{1,0:T(8,128)(2,1)S(1)} %collective-permute-done.1.refs_0_) | copy-start | bytes 393220
  251.8 8.6 %collective-permute-start.2 = (bf16[256,256]{1,0:T(8,128)(2,1)S(1)}, bf16[256,256]{1,0:T(8,128)(2,1)S(1)}, u32[]{:S(2)}, u32[]{:S(2)}) collective-permute-start(bf16[256,256]{1,0:T(8,128)(2,1)S(1)} %copy-done.37), channel_id=1, source_target_pairs={{0,4},{1,5},{2,6},{3,7},{4,0},{5,1},{6,2},{7,3},{8,12},{9,13},{10,... | collective-permute-start | bytes 393224 | tf_op jit(solution)/shard_map/ppermute | solution.py:240
  260.4 5.4 %copy-start.34 = (bf16[256,256]{1,0:T(8,128)(2,1)}, bf16[256,256]{1,0:T(8,128)(2,1)S(1)}, u32[]{:S(2)}) copy-start(bf16[256,256]{1,0:T(8,128)(2,1)S(1)} %collective-permute-done.2.refs_1_) | copy-start | bytes 393220
  260.4 5.4 %collective-permute-start.3 = (bf16[256,256]{1,0:T(8,128)(2,1)S(1)}, bf16[256,256]{1,0:T(8,128)(2,1)S(1)}, u32[]{:S(2)}, u32[]{:S(2)}) collective-permute-start(bf16[256,256]{1,0:T(8,128)(2,1)S(1)} %copy-done.36), channel_id=1, source_target_pairs={{0,6},{1,7},{2,0},{3,1},{4,2},{5,3},{6,4},{7,5},{8,14},{9,15},{10,... | collective-permute-start | bytes 393224 | tf_op jit(solution)/shard_map/ppermute | solution.py:240
  269.4 7.1 %collective-permute-start.12 = (bf16[256,256]{1,0:T(8,128)(2,1)}, bf16[256,256]{1,0:T(8,128)(2,1)S(1)}, u32[]{:S(2)}, u32[]{:S(2)}) collective-permute-start(bf16[256,256]{1,0:T(8,128)(2,1)} %get-tuple-element.47.refs_0_), channel_id=1, source_target_pairs={{0,2},{1,3},{2,4},{3,5},{4,6},{5,7},{6,0},{7,1},{8,10},{9,11},{10,... | collective-permute-start | bytes 393224 | tf_op jit(solution)/shard_map/ppermute | solution.py:240
  276.6 19.8 %copy-start.19 = (bf16[256,256]{1,0:T(8,128)(2,1)}, bf16[256,256]{1,0:T(8,128)(2,1)S(1)}, u32[]{:S(2)}) copy-start(bf16[256,256]{1,0:T(8,128)(2,1)S(1)} %collective-permute-done.12.refs_1_) | copy-start | bytes 393220
  276.6 8.6 %collective-permute-start.13 = (bf16[256,256]{1,0:T(8,128)(2,1)}, bf16[256,256]{1,0:T(8,128)(2,1)S(1)}, u32[]{:S(2)}, u32[]{:S(2)}) collective-permute-start(bf16[256,256]{1,0:T(8,128)(2,1)} %get-tuple-element.47.refs_0_), channel_id=1, source_target_pairs={{0,4},{1,5},{2,6},{3,7},{4,0},{5,1},{6,2},{7,3},{8,12},{9,13},{10,... | collective-permute-start | bytes 393224 | tf_op jit(solution)/shard_map/ppermute | solution.py:240
  285.1 11.2 %copy-start.21 = (bf16[256,256]{1,0:T(8,128)(2,1)}, bf16[256,256]{1,0:T(8,128)(2,1)S(1)}, u32[]{:S(2)}) copy-start(bf16[256,256]{1,0:T(8,128)(2,1)S(1)} %collective-permute-done.13.refs_2_) | copy-start | bytes 393220
  285.1 5.6 %collective-permute-start.14 = (bf16[256,256]{1,0:T(8,128)(2,1)}, bf16[256,256]{1,0:T(8,128)(2,1)S(1)}, u32[]{:S(2)}, u32[]{:S(2)}) collective-permute-start(bf16[256,256]{1,0:T(8,128)(2,1)} %get-tuple-element.47.refs_0_), channel_id=1, source_target_pairs={{0,6},{1,7},{2,0},{3,1},{4,2},{5,3},{6,4},{7,5},{8,14},{9,15},{10,... | collective-permute-start | bytes 393224 | tf_op jit(solution)/shard_map/ppermute | solution.py:240
  290.7 5.6 %copy-start.22 = (bf16[256,256]{1,0:T(8,128)(2,1)}, bf16[256,256]{1,0:T(8,128)(2,1)S(1)}, u32[]{:S(2)}) copy-start(bf16[256,256]{1,0:T(8,128)(2,1)S(1)} %collective-permute-done.14.refs_3_) | copy-start | bytes 393220
  290.7 1.6 collective-permute-start.15
  292.3 4.1 %copy-start.23 = (bf16[256,256]{1,0:T(8,128)(2,1)}, bf16[256,256]{1,0:T(8,128)(2,1)S(1)}, u32[]{:S(2)}) copy-start(bf16[256,256]{1,0:T(8,128)(2,1)S(1)} %collective-permute-done.15.refs_4_) | copy-start | bytes 393220
  292.3 1.3 collective-permute-start.16
  293.6 2.7 copy-start.24
  293.6 1.3 collective-permute-start.17
  295.0 1.4 copy-start.25
  295.0 1.3 collective-permute-start.18
  297.0 1.3 copy-start.9
  309.8 1.4 copy-start.8
  322.8 1.3 copy-start.7
  (13 other events, 9.1 us)

commit v2 on v0

v2 whole, which is shorter than its diff:
```python
import functools

import jax
import jax.numpy as jnp
from jax import lax
from jax.experimental import pallas as pl
from jax.experimental.pallas import tpu as pltpu
from jax.sharding import PartitionSpec as P

MIB = 2**20
HASTE = 0.4
HBM = pl.BlockSpec(memory_space=pl.ANY)
FAST = pl.BlockSpec(memory_space=pltpu.VMEM)
WORDS = pl.BlockSpec(memory_space=pltpu.SMEM)
BF16, F32 = jnp.bfloat16, jnp.float32


def cost(flops, nbytes):
    return pl.CostEstimate(flops=int(flops * HASTE), bytes_accessed=int(nbytes * HASTE), transcendentals=0)


LIMITS = {"flows": 26, "pair_sum": 26, "overload": 26, "sens": 26, "add_last": 26}


def call(body, name, out_shape, in_specs, out_specs, scratch, estimate, aliases={}):
    return pl.pallas_call(
        body,
        out_shape=out_shape,
        in_specs=in_specs,
        out_specs=out_specs,
        scratch_shapes=scratch,
        input_output_aliases=aliases,
        compiler_params=pltpu.CompilerParams(vmem_limit_bytes=LIMITS[name] * MIB),
        cost_estimate=estimate,
        name=name,
    )


def resident(x):
    return pltpu.with_memory_space_constraint(x, pltpu.VMEM)


def at(index, size):
    return pl.ds(pl.multiple_of(index * size, size), size)


def penalty_and_adjoint(flows, limits):
    magnitude = jnp.sqrt(flows * flows + 1.0)
    zvalue = 4.0 * (magnitude / limits - 1.0)
    penalty = (jnp.maximum(zvalue, 0.0) + jnp.log1p(jnp.exp(-jnp.abs(zvalue)))) * 0.25
    adjoint = jax.nn.sigmoid(zvalue) * flows / (magnitude * limits)
    return penalty, adjoint


def flows_kernel(first, bounds, depth, block, pos, slab, codes, *refs):
    refs = list(refs)
    before = refs.pop(0) if bounds[0] > 0 else None
    held = refs.pop(0) if first else slab
    last = bounds[1] * depth == held.shape[1]
    outs = [refs.pop(0), refs.pop(0)] if last else []
    total = refs.pop(0)
    drawn, code_sem = refs.pop(0), refs.pop(0)
    slab_sem = refs.pop(0) if first else None
    out_sem = refs.pop(0) if last else None
    rows, hours = total.shape
    lo, hi = bounds

    def fetch(j):
        copies = [
            pltpu.make_async_copy(
                codes.at[at(j, depth), at(pos[block], hours)], drawn.at[j - lo], code_sem.at[j - lo]
            )
        ]
        if first:
            cols = at(j, depth)
            copies.append(pltpu.make_async_copy(slab.at[:, cols], held.at[:, cols], slab_sem.at[j]))
        return copies

    for j in range(lo, hi):
        for copy in fetch(j):
            copy.start()

    own = rows // 8
    stores = []

    def leave(chip):
        for side, core in ((0, pos[1]), (1, 1 - pos[1])):
            stores.append(
                pltpu.make_async_copy(
                    total.at[at(2 * chip + core, own), :],
                    outs[side].at[chip * own : (chip + 1) * own, :],
                    out_sem.at[2 * chip + side],
                )
            )
            stores[-1].start()

    def step(j, add, final=False):
        for copy in fetch(j):
            copy.wait()
        injections = (drawn[j - lo].astype(F32) * (1.0 / 1024.0)).astype(BF16)
        for chip in range(4):
            here = slice(2 * chip * own, 2 * (chip + 1) * own)
            part = jnp.dot(held[here, at(j, depth)], injections, preferred_element_type=F32)
            total[here, :] = part if add is None else add[here, :] + part
            if final:
                leave(chip)

    step(lo, before)

    @pl.loop(lo + 1, hi - last)
    def _(j):
        step(j, total)

    if last:
        step(hi - 1, total, True)
        for copy in stores:
            copy.wait()


def partial_flows(pos, slab, codes, block, hours, first=False, bounds=None, before=None):
    rows, buses = slab.shape
    depth = min(512, buses)
    steps = buses // depth
    bounds = bounds or (0, steps)
    last = bounds[1] == steps
    count = bounds[1] - bounds[0]
    out_shape, out_specs = [], []
    if first:
        out_shape, out_specs = [pltpu.VMEM(slab.shape, BF16)], [FAST]
    scratch = []
    if last:
        out_shape += [jax.ShapeDtypeStruct((rows // 2, hours), F32)] * 2
        out_specs += [HBM] * 2
        scratch.append(pltpu.VMEM((rows, hours), F32))
    else:
        out_shape.append(pltpu.VMEM((rows, hours), F32))
        out_specs.append(FAST)
    scratch += [pltpu.VMEM((count, depth, hours), jnp.int32), pltpu.SemaphoreType.DMA((count,))]
    if first:
        scratch.append(pltpu.SemaphoreType.DMA((count,)))
    else:
        slab = resident(slab)
    if last:
        scratch.append(pltpu.SemaphoreType.DMA((8,)))
    operands = [pos, slab, codes]
    in_specs = [WORDS, HBM if first else FAST, HBM]
    if before is not None:
        operands.append(resident(before))
        in_specs.append(FAST)
    return call(
        functools.partial(flows_kernel, first, bounds, depth, block),
        "flows",
        out_shape,
        in_specs,
        out_specs,
        scratch,
        cost(2 * rows * count * depth * hours, (2 * rows if first else 4 * hours) * count * depth),
    )(*operands)


def pair_kernel(pos, slab, keep, came, *refs):
    outs, (a, b, mine, sends, in_sem, out_sem) = refs[:4], refs[4:]
    own = mine.shape[0]
    copies, done = [], []
    for k in range(4):
        rows = at(lax.rem(pos[0] + k, 4), own)
        for n, (src, dst) in enumerate(((keep, a), (came, b))):
            copies.append(pltpu.make_async_copy(src.at[rows, :], dst.at[k], in_sem.at[2 * k + n]))
            copies[-1].start()
    for k in (1, 2, 3, 0):
        copies[2 * k].wait()
        copies[2 * k + 1].wait()
        both = a[k] + b[k]
        if k:
            sends[k - 1] = both.astype(BF16)
        else:
            mine[...] = both
        done.append(pltpu.make_async_copy(sends.at[k - 1] if k else mine, outs[k], out_sem.at[k]))
        done[-1].start()
    for copy in done:
        copy.wait()


def pair_sum(pos, slab, keep, came):
    rows, hours = keep.shape
    own = rows // 4
    shard = jax.ShapeDtypeStruct((own, hours), BF16)
    return call(
        pair_kernel,
        "pair_sum",
        [jax.ShapeDtypeStruct((own, hours), F32)] + [shard] * 3,
        [WORDS, FAST, HBM, HBM],
        [HBM] * 4,
        [
            pltpu.VMEM((4, own, hours), F32),
            pltpu.VMEM((4, own, hours), F32),
            pltpu.VMEM((own, hours), F32),
            pltpu.VMEM((3, own, hours), BF16),
            pltpu.SemaphoreType.DMA((8,)),
            pltpu.SemaphoreType.DMA((4,)),
        ],
        cost(rows * hours, 10 * rows * hours),
    )(pos, resident(slab), keep, came)


def overload_kernel(others, block, parts, part, pos, slab, codes, mine, *refs):
    came, refs = refs[:others], refs[others:]
    penalty, adjoint, held, got, drawn, pen, adj, in_sem, out_sem = refs[-9:]
    own, hours = mine.shape
    copies = [
        pltpu.make_async_copy(codes, drawn, in_sem.at[0]),
        pltpu.make_async_copy(mine, held, in_sem.at[1]),
    ]
    for n in range(others):
        copies.append(pltpu.make_async_copy(came[n], got.at[n], in_sem.at[2 + n]))
    for copy in copies:
        copy.start()
    for copy in copies:
        copy.wait()
    flows = held[...]
    for n in range(others):
        flows += got[n].astype(F32)
    lines = own // drawn.shape[1]
    first = (2 * pos[0] + pos[1]) * lines
    limits = jnp.concatenate([drawn[pl.ds(first + n, 1), :] for n in range(lines)], 1).astype(F32) / 64.0
    value, slope = penalty_and_adjoint(flows.T, limits)
    adj[...] = slope.astype(BF16)
    send = pltpu.make_async_copy(adj, adjoint, out_sem.at[0])
    send.start()
    pen[...] = value.T
    cols = at(pos[block] * parts + part, hours)
    store = pltpu.make_async_copy(pen, penalty.at[:, cols], out_sem.at[1])
    store.start()
    send.wait()
    store.wait()


def overload(pos, slab, codes, mine, came, penalty, hours_all, block, parts=1, part=0):
    own, hours = mine.shape
    operands = [pos, resident(slab), codes, mine, *came]
    aliases = {}
    if penalty is not None:
        aliases = {len(operands): 0}
        operands.append(penalty)
    return call(
        functools.partial(overload_kernel, len(came), block, parts, part),
        "overload",
        (jax.ShapeDtypeStruct((own, hours_all), F32), jax.ShapeDtypeStruct((hours, own), BF16)),
        [WORDS, FAST] + [HBM] * (len(operands) - 2),
        (HBM, HBM),
        [
            pltpu.VMEM((own, hours), F32),
            pltpu.VMEM((3, own, hours), BF16),
            pltpu.VMEM(codes.shape, jnp.int32),
            pltpu.VMEM((own, hours), F32),
            pltpu.VMEM((hours, own), BF16),
            pltpu.SemaphoreType.DMA((5,)),
            pltpu.SemaphoreType.DMA((2,)),
        ],
        cost(20 * mine.size, 16 * mine.size),
        aliases=aliases,
    )(*operands)


def sens_kernel(halves, block, adds, pos, slab, *refs):
    shards, refs = refs[:8], refs[8:]
    extra, refs = refs[:adds], refs[adds:]
    outs, (adjoint, got, made, shard_sem, got_sem, out_sem) = refs[: len(halves)], refs[len(halves) :]
    rows = adjoint.shape[1]
    own = rows // 8
    steps = made.shape[0] // len(halves)
    copies = []
    for k in range(8):
        slot = 2 * lax.rem(pos[0] + 4 - k % 4, 4) + (pos[1] if k < 4 else 1 - pos[1])
        copies.append(pltpu.make_async_copy(shards[k], adjoint.at[:, at(slot, own)], shard_sem.at[k]))
    arrivals = [pltpu.make_async_copy(extra[n], got.at[n], got_sem.at[n]) for n in range(adds)]
    for copy in copies + arrivals:
        copy.start()
    for copy in copies:
        copy.wait()

    def store(n, i):
        return pltpu.make_async_copy(made.at[n * steps + i], outs[n].at[:, at(i, block)], out_sem.at[n * steps + i])

    for n, half in enumerate(halves):
        if adds:
            arrivals[n].wait()

        @pl.loop(0, steps)
        def _(i):
            part = jnp.dot(adjoint[...], slab[:, at(half * steps + i, block)], preferred_element_type=F32)
            if adds:
                part += got[n, :, at(i, block)].astype(F32)
            made[n * steps + i] = part.astype(made.dtype)
            store(n, i).start()

    for n in range(len(halves)):
        for i in range(steps):
            store(n, i).wait()


def partial_sens(pos, slab, shards, halves, adds=(), dtype=BF16):
    rows, buses = slab.shape
    hours = shards[0].shape[0]
    block = min(1024, buses // 2)
    steps = buses // 2 // block * len(halves)
    return call(
        functools.partial(sens_kernel, halves, block, len(adds)),
        "sens",
        [jax.ShapeDtypeStruct((hours, buses // 2), dtype)] * len(halves),
        [WORDS, FAST] + [HBM] * (8 + len(adds)),
        [HBM] * len(halves),
        [
            pltpu.VMEM((hours, rows), BF16),
            pltpu.VMEM((len(adds), hours, buses // 2) if adds else (1, 16, 128), BF16),
            pltpu.VMEM((steps, hours, block), dtype),
            pltpu.SemaphoreType.DMA((8,)),
            pltpu.SemaphoreType.DMA((max(1, len(adds)),)),
            pltpu.SemaphoreType.DMA((steps,)),
        ],
        cost(rows * buses * hours * len(halves), buses * hours * len(halves)),
    )(pos, resident(slab), *shards, *adds)


def add_kernel(half, block, total, came, *refs):
    out, a, b, c, in_sem, out_sem = refs[-6:]
    steps = a.shape[0]

    def fetch(i):
        cols = at(i, block)
        return (
            pltpu.make_async_copy(total.at[:, cols], a.at[i], in_sem.at[0, i]),
            pltpu.make_async_copy(came.at[:, cols], b.at[i], in_sem.at[1, i]),
        )

    def store(i):
        return pltpu.make_async_copy(c.at[i], out.at[at(half * steps + i, block), :], out_sem.at[i])

    for i in range(steps):
        for copy in fetch(i):
            copy.start()

    @pl.loop(0, steps)
    def _(i):
        for copy in fetch(i):
            copy.wait()
        c[i] = (a[i] + b[i].astype(F32)).T
        store(i).start()

    for i in range(steps):
        store(i).wait()


def add_last(total, came, half, into):
    hours, buses = total.shape
    block = min(512, buses)
    steps = buses // block
    operands = [total, came] + ([] if into is None else [into])
    return call(
        functools.partial(add_kernel, half, block),
        "add_last",
        jax.ShapeDtypeStruct((2 * buses, hours), F32),
        [HBM] * len(operands),
        HBM,
        [
            pltpu.VMEM((steps, hours, block), F32),
            pltpu.VMEM((steps, hours, block), BF16),
            pltpu.VMEM((steps, block, hours), F32),
            pltpu.SemaphoreType.DMA((2, steps)),
            pltpu.SemaphoreType.DMA((steps,)),
        ],
        cost(came.size, 10 * came.size),
        aliases={} if into is None else {2: 0},
    )(*operands)


def local_tree(ptdf, load_codes, limit_codes):
    rows, buses = ptdf.shape
    hours_all = load_codes.shape[1]
    wide = hours_all // 4
    me, spot = lax.axis_index("br"), lax.axis_index("bus")
    pos = jnp.stack([spot // 2, spot % 2, me ^ 3, me ^ 1, me ^ 2, me]).astype(jnp.int32)
    limits = limit_codes.reshape(rows // 128, 128)
    far, over, up, home = 2, 3, 4, 5
    order = [pos]

    def run(kernel, *operands, **options):
        out = kernel(order[0], *operands, **options)
        order[0], _ = lax.optimization_barrier((order[0], jax.tree.leaves(out)[-1]))
        return out

    def across(x, bit):
        return lax.ppermute(x, "br", [(i, i ^ bit) for i in range(4)])

    def swap(x):
        return lax.ppermute(x, "bus", [(i, i ^ 1) for i in range(8)])

    def chip_ahead(x, k):
        return lax.ppermute(x, "bus", [(i, (i + 2 * k) % 8) for i in range(8)])

    def flows(block, **options):
        return run(partial_flows, slab, load_codes, block, wide, **options)

    def gate(x):
        return lax.optimization_barrier((x, order[0]))[0]

    def pair(keep, away):
        mine, *sends = run(pair_sum, slab, keep, swap(gate(away)))
        return mine, [chip_ahead(x, k + 1) for k, x in enumerate(sends)]

    penalty = None

    def adjoints(flow, block):
        nonlocal penalty
        mine, came = flow
        penalty, adjoint = run(overload, slab, limits, mine, came, penalty, hours_all, block)
        return [adjoint] + [chip_ahead(adjoint, k) for k in (1, 2, 3)]

    def shared(shards):
        return shards + [swap(gate(x)) for x in shards]

    def sens(shards, halves, **options):
        return run(partial_sens, slab, shards, halves, **options)

    def arrived(*xs):
        order[0], *_ = lax.optimization_barrier((order[0], *xs))

    slab = ptdf
    slab, keep, away = flows(far, first=True)
    flow_far = pair(keep, away)
    over_parts = flows(over)
    adj_far = adjoints(flow_far, far)
    flow_over = pair(*over_parts)
    up_parts = flows(up)
    far_a, far_b = sens(shared(adj_far), (0, 1))
    far_a, far_b = across(far_a, 1), across(far_b, 2)
    adj_over = adjoints(flow_over, over)
    flow_up = pair(*up_parts)
    home_parts = flows(home)
    adj_up = adjoints(flow_up, up)
    adj_over = shared(adj_over)
    over_a = across(sens(adj_over, (0,))[0], 1)
    flow_home = pair(*home_parts)
    adj_up = shared(adj_up)
    up_b = across(sens(adj_up, (1,))[0], 2)
    arrived(far_a, far_b)
    over_b = across(sens(adj_over, (1,), adds=(far_b,))[0], 1)
    up_a = across(sens(adj_up, (0,), adds=(far_a,))[0], 2)
    adj_home = adjoints(flow_home, home)
    total_a, total_b = sens(shared(adj_home), (0, 1), adds=(over_a, up_b), dtype=F32)
    total = add_last(total_b, over_b, 1, None)
    return penalty, add_last(total_a, up_a, 0, total)


def local_general(ptdf, load_codes, limit_codes):
    own = ptdf.shape[0] // lax.axis_size("bus")
    injections = (load_codes.astype(F32) / 1024.0).astype(BF16)
    flows = lax.psum_scatter(
        jnp.dot(ptdf, injections, preferred_element_type=F32), "bus", scatter_dimension=0, tiled=True
    )
    codes = lax.dynamic_slice_in_dim(limit_codes, lax.axis_index("bus") * own, own, 0)
    penalty, mine = penalty_and_adjoint(flows, codes.astype(F32)[:, None] / 64.0)
    adjoint = lax.all_gather(mine.astype(BF16), "bus", axis=0, tiled=True)
    part = lax.dot_general(ptdf, adjoint, (((0,), (0,)), ((), ())), preferred_element_type=F32)
    return penalty, lax.psum_scatter(part, "br", scatter_dimension=1, tiled=True)


def solution(mesh):
    tree = mesh.shape["br"] == 4 and mesh.shape["bus"] == 8
    return jax.shard_map(
        local_tree if tree else local_general,
        mesh=mesh,
        in_specs=(P("br", "bus"), P("bus", None), P("br")),
        out_specs=(P(("br", "bus"), None), P("bus", "br")),
        check_vma=False,
    )
```

time: 596 us -> 272 us (0.46)
  waiting for transfers between devices: 459 us -> 63.6 us
  Pallas kernels: 0 us -> 151 us
  matrix products: 105 us -> 0 us
  starting transfers between devices: 0.26 us -> 42.3 us
  between operations: 14.1 us -> 1.61 us
  other arithmetic: 6.31 us -> 0 us
    reduce_scatter x1 -> x0, waiting for transfers between devices: 281 us -> none  [local(): lax.psum_scatter(partial_sens, 'br', scatter_dimension=1, tiled=True)]
    psum x1 -> x0, waiting for transfers between devices: 178 us -> none  [local(): flows = lax.psum(partial_flows, 'bus')]
    pallas_call x0 -> x20, Pallas kernels: none -> 151 us  [the longest x4 60.1 us: partial_flows(): call(functools.partial(flows_kernel, first, bounds, depth, block), 'flows...]
    dot_general x2 -> x0, matrix products: 105 us -> none  [the longest x1 61.7 us: local(): lax.dot_general(ptdf, adjoint_block, (((0,), (0,)), ((), ())), preferred_...]
    ppermute x0 -> x50, waiting for transfers between devices: none -> 63.6 us  [the longest x24 47.7 us: chip_ahead(): return lax.ppermute(x, 'bus', [(i, (i + 2 * k) % 8) for i in range(8)])]
    ppermute x0 -> x50, starting transfers between devices: none -> 42.3 us  [the longest x24 30.8 us: chip_ahead(): return lax.ppermute(x, 'bus', [(i, (i + 2 * k) % 8) for i in range(8)])]
    unnamed x4 -> x118, local copies, waits for them, and re-layouts: 10.7 us -> 13.1 us
  transfers between devices with their start and end apart: 2 -> 50, of which waited for: 2 -> 21; matrix products, arithmetic and copies ran while one was open for 1% -> 0% of each run, Pallas kernels for 0% -> 44%
where the time goes in v2:
time: 272 us
  Pallas kernels  151 us (56%)
  waiting for transfers between devices  63.6 us (23%)
  starting transfers between devices  42.3 us (16%)
  local copies, waits for them, and re-layouts  13.8 us (5%)
    pallas_call x4, Pallas kernels, partial_flows(): call(functools.partial(flows_kernel, first, bounds, depth, block), 'flows...  60.1 us
    pallas_call x6, Pallas kernels, partial_sens(): call(functools.partial(sens_kernel, halves, block, len(adds)), 'sens', [j...  59.3 us
    ppermute x24, waiting for transfers between devices, chip_ahead(): return lax.ppermute(x, 'bus', [(i, (i + 2 * k) % 8) for i in range(8)])  47.7 us
    ppermute x24, starting transfers between devices, chip_ahead(): return lax.ppermute(x, 'bus', [(i, (i + 2 * k) % 8) for i in range(8)])  30.8 us
    ppermute x20, waiting for transfers between devices, swap(): return lax.ppermute(x, 'bus', [(i, i ^ 1) for i in range(8)])  13.9 us
    unnamed x118, local copies, waits for them, and re-layouts  13.1 us
    pallas_call x4, Pallas kernels, pair_sum(): call(pair_kernel, 'pair_sum', [jax.ShapeDtypeStruct((own, hours), F32)] +...  12.4 us
    pallas_call x4, Pallas kernels, overload(): call(functools.partial(overload_kernel, len(came), block, parts, part), '...  12.3 us
  transfers between devices with their start and end apart: 50, of which 21 were waited for; matrix products, arithmetic and copies ran while one was open for 0% of the time, Pallas kernels for 44%

profile of v2, /device:TPU:0, one launch (start us, length us, event | category | flops | bytes accessed | tf_op | source)
XLA Modules:
  0.0 271.8 jit_solution(47733408868653236)
XLA Ops:
  0.6 0.7 stack.27.pos
  1.3 16.1 %flows.4 = (bf16[2048,8192]{1,0:T(8,128)(2,1)S(1)}, f32[1024,256]{1,0:T(8,128)}, f32[1024,256]{1,0:T(8,128)}) custom-call(s32[6]{0:T(128)} %stack.27.pos, bf16[2048,8192]{1,0:T(8,128)(2,1)} %slab.1, s32[8192,1024]{1,0:T(8,128)} %codes.7), custom_call_target="tpu_custom_call" | custom-call | flops 3435973888 | bytes 13421772 | tf_op jit(solution)/shard_map/flows/pallas_call | solution.py:150
  18.0 2.5 collective-permute-done.came
  20.5 1.0 copy-done.6
  21.4 3.1 %pair_sum.4 = (f32[256,256]{1,0:T(8,128)}, bf16[256,256]{1,0:T(8,128)(2,1)}, bf16[256,256]{1,0:T(8,128)(2,1)}, bf16[256,256]{1,0:T(8,128)(2,1)}) custom-call(s32[6]{0:T(128)} %stack.27.pos, bf16[2048,8192]{1,0:T(8,128)(2,1)S(1)} %get-tuple-element.79.slab, f32[1024,256]{1,0:T(8,128)} %get-tuple-element.80.keep, f32[1024,256]{1,0:T(8,128)} %copy-done.6), custom_call_target="tpu_custom_call" | custom-call | flops 104857 | bytes 1048576 | tf_op jit(solution)/shard_map/pair_sum/pallas_call | solution.py:188
  24.5 5.0 %collective-permute-start.3 = (bf16[256,256]{1,0:T(8,128)(2,1)}, bf16[256,256]{1,0:T(8,128)(2,1)S(1)}, u32[]{:S(2)}, u32[]{:S(2)}) collective-permute-start(bf16[256,256]{1,0:T(8,128)(2,1)} %get-tuple-element.82), channel_id=1, source_target_pairs={{0,6},{1,7},{2,0},{3,1},{4,2},{5,3},{6,4},{7,5},{8,14},{9,15},{10,... | collective-permute-start | bytes 393224 | tf_op jit(solution)/shard_map/ppermute | solution.py:399
  29.5 1.0 collective-permute-start.2
  30.5 14.6 %flows.5 = (f32[1024,256]{1,0:T(8,128)}, f32[1024,256]{1,0:T(8,128)}) custom-call(s32[6]{0:T(128)} %stack.27.pos, bf16[2048,8192]{1,0:T(8,128)(2,1)S(1)} %get-tuple-element.79.slab, s32[8192,1024]{1,0:T(8,128)} %codes.7), custom_call_target="tpu_custom_call" | custom-call | flops 3435973888 | bytes 3355443 | tf_op jit(solution)/shard_map/flows/pallas_call | solution.py:150
  45.9 3.2 %overload.4 = (f32[256,1024]{1,0:T(8,128)}, bf16[256,256]{1,0:T(8,128)(2,1)}) custom-call(s32[6]{0:T(128)} %stack.27.pos, bf16[2048,8192]{1,0:T(8,128)(2,1)S(1)} %get-tuple-element.79.slab, s32[16,128]{1,0:T(8,128)} %bitcast.7, f32[256,256]{1,0:T(8,128)} %get-tuple-element.86.mine, bf16[256,256]{1,0:T(8,128)(2,1)} %copy-done.46, ...), custom_call_target="tpu_custom_call" | custom-call | flops 524288 | bytes 419430 | tf_op jit(solution)/shard_map/overload/pallas_call | solution.py:245
  49.2 2.9 %collective-permute-start.7 = (bf16[256,256]{1,0:T(8,128)(2,1)}, bf16[256,256]{1,0:T(8,128)(2,1)S(1)}, u32[]{:S(2)}, u32[]{:S(2)}) collective-permute-start(bf16[256,256]{1,0:T(8,128)(2,1)} %get-tuple-element.97.refs_0_), channel_id=1, source_target_pairs={{0,6},{1,7},{2,0},{3,1},{4,2},{5,3},{6,4},{7,5},{8,14},{9,15},{10,... | collective-permute-start | bytes 393224 | tf_op jit(solution)/shard_map/ppermute | solution.py:399
  52.0 2.0 collective-permute-start.6
  54.1 1.0 copy-done.4
  55.1 3.0 %pair_sum.5 = (f32[256,256]{1,0:T(8,128)}, bf16[256,256]{1,0:T(8,128)(2,1)}, bf16[256,256]{1,0:T(8,128)(2,1)}, bf16[256,256]{1,0:T(8,128)(2,1)}) custom-call(s32[6]{0:T(128)} %stack.27.pos, bf16[2048,8192]{1,0:T(8,128)(2,1)S(1)} %get-tuple-element.79.slab, f32[1024,256]{1,0:T(8,128)} %get-tuple-element.91.keep, f32[1024,256]{1,0:T(8,128)} %copy-done.4), custom_call_target="tpu_custom_call" | custom-call | flops 104857 | bytes 1048576 | tf_op jit(solution)/shard_map/pair_sum/pallas_call | solution.py:188
  58.2 14.8 %flows.6 = (f32[1024,256]{1,0:T(8,128)}, f32[1024,256]{1,0:T(8,128)}) custom-call(s32[6]{0:T(128)} %stack.27.pos, bf16[2048,8192]{1,0:T(8,128)(2,1)S(1)} %get-tuple-element.79.slab, s32[8192,1024]{1,0:T(8,128)} %codes.7), custom_call_target="tpu_custom_call" | custom-call | flops 3435973888 | bytes 3355443 | tf_op jit(solution)/shard_map/flows/pallas_call | solution.py:150
  74.1 3.8 %collective-permute-start.14 = (bf16[256,256]{1,0:T(8,128)(2,1)S(1)}, bf16[256,256]{1,0:T(8,128)(2,1)S(1)}, u32[]{:S(2)}, u32[]{:S(2)}) collective-permute-start(bf16[256,256]{1,0:T(8,128)(2,1)S(1)} %copy-done.56), channel_id=1, source_target_pairs={{0,6},{1,7},{2,0},{3,1},{4,2},{5,3},{6,4},{7,5},{8,14},{9,15},{10,... | collective-permute-start | bytes 393224 | tf_op jit(solution)/shard_map/ppermute | solution.py:399
  78.0 0.9 collective-permute-start.13
  79.5 0.6 copy-done.41
  80.2 12.9 %sens.6 = (bf16[256,4096]{1,0:T(8,128)(2,1)}, bf16[256,4096]{1,0:T(8,128)(2,1)}) custom-call(s32[6]{0:T(128)} %stack.27.pos, bf16[2048,8192]{1,0:T(8,128)(2,1)S(1)} %get-tuple-element.79.slab, bf16[256,256]{1,0:T(8,128)(2,1)} %get-tuple-element.97.refs_0_, bf16[256,256]{1,0:T(8,128)(2,1)} %copy-done.27, bf16[256,256]{1,0:T(8,128)(2,1)} %copy-done.26, ...), custom_call_target="tpu_custom_call" | custom-call | flops 3435973888 | bytes 1677721 | tf_op jit(solution)/shard_map/sens/pallas_call | solution.py:307
  93.9 3.2 %overload.5 = (f32[256,1024]{1,0:T(8,128)}, bf16[256,256]{1,0:T(8,128)(2,1)}) custom-call(s32[6]{0:T(128)} %stack.27.pos, bf16[2048,8192]{1,0:T(8,128)(2,1)S(1)} %get-tuple-element.79.slab, s32[16,128]{1,0:T(8,128)} %bitcast.8, f32[256,256]{1,0:T(8,128)} %get-tuple-element.103.mine, bf16[256,256]{1,0:T(8,128)(2,1)} %copy-done.34, ...), custom_call_target="tpu_custom_call", output_to_operand_aliasing={{0}: (7, {})} | custom-call | flops 524288 | bytes 419430 | tf_op jit(solution)/shard_map/overload/pallas_call | solution.py:245
  97.2 2.6 collective-permute-done.15.came
  99.8 1.0 copy-done.7
  100.8 3.2 %pair_sum.6 = (f32[256,256]{1,0:T(8,128)}, bf16[256,256]{1,0:T(8,128)(2,1)}, bf16[256,256]{1,0:T(8,128)(2,1)}, bf16[256,256]{1,0:T(8,128)(2,1)}) custom-call(s32[6]{0:T(128)} %stack.27.pos, bf16[2048,8192]{1,0:T(8,128)(2,1)S(1)} %get-tuple-element.79.slab, f32[1024,256]{1,0:T(8,128)} %get-tuple-element.109.keep, f32[1024,256]{1,0:T(8,128)} %copy-done.7), custom_call_target="tpu_custom_call" | custom-call | flops 104857 | bytes 1048576 | tf_op jit(solution)/shard_map/pair_sum/pallas_call | solution.py:188
  104.1 3.6 %collective-permute-start.16 = (bf16[256,256]{1,0:T(8,128)(2,1)}, bf16[256,256]{1,0:T(8,128)(2,1)S(1)}, u32[]{:S(2)}, u32[]{:S(2)}) collective-permute-start(bf16[256,256]{1,0:T(8,128)(2,1)} %get-tuple-element.116), channel_id=1, source_target_pairs={{0,2},{1,3},{2,4},{3,5},{4,6},{5,7},{6,0},{7,1},{8,10},{9,11},{10,... | collective-permute-start | bytes 393224 | tf_op jit(solution)/shard_map/ppermute | solution.py:399
  107.9 1.5 collective-permute-start.35
  109.5 1.5 collective-permute-start.34
  110.9 1.2 collective-permute-start.18
  112.5 1.7 collective-permute-start.17
  114.2 14.7 %flows.7 = (f32[1024,256]{1,0:T(8,128)}, f32[1024,256]{1,0:T(8,128)}) custom-call(s32[6]{0:T(128)} %stack.27.pos, bf16[2048,8192]{1,0:T(8,128)(2,1)S(1)} %get-tuple-element.79.slab, s32[8192,1024]{1,0:T(8,128)} %codes.7), custom_call_target="tpu_custom_call" | custom-call | flops 3435973888 | bytes 3355443 | tf_op jit(solution)/shard_map/flows/pallas_call | solution.py:150
  128.9 1.3 collective-permute-start.20
  130.1 1.8 collective-permute-start.19
  131.9 3.0 %overload.6 = (f32[256,1024]{1,0:T(8,128)}, bf16[256,256]{1,0:T(8,128)(2,1)}) custom-call(s32[6]{0:T(128)} %stack.27.pos, bf16[2048,8192]{1,0:T(8,128)(2,1)S(1)} %get-tuple-element.79.slab, s32[16,128]{1,0:T(8,128)} %bitcast.9, f32[256,256]{1,0:T(8,128)} %get-tuple-element.115.mine, bf16[256,256]{1,0:T(8,128)(2,1)} %copy-done.30, ...), custom_call_target="tpu_custom_call", output_to_operand_aliasing={{0}: (7, {})} | custom-call | flops 524288 | bytes 419430 | tf_op jit(solution)/shard_map/overload/pallas_call | solution.py:245
  135.1 4.0 %collective-permute-done.20.refs_2_ = bf16[256,256]{1,0:T(8,128)(2,1)S(1)} collective-permute-done((bf16[256,256]{1,0:T(8,128)(2,1)S(1)}, bf16[256,256]{1,0:T(8,128)(2,1)S(1)}, u32[]{:S(2)}, u32[]{:S(2)}) %collective-permute-start.20) | collective-permute-done | bytes 131104 | tf_op jit(solution)/shard_map/ppermute | solution.py:399
  139.7 0.8 collective-permute-done.23.refs_5_
  141.3 0.6 copy-done.16
  142.0 7.9 %sens.7 = bf16[256,4096]{1,0:T(8,128)(2,1)} custom-call(s32[6]{0:T(128)} %stack.27.pos, bf16[2048,8192]{1,0:T(8,128)(2,1)S(1)} %get-tuple-element.79.slab, bf16[256,256]{1,0:T(8,128)(2,1)} %get-tuple-element.121.refs_0_, bf16[256,256]{1,0:T(8,128)(2,1)} %copy-done.12, bf16[256,256]{1,0:T(8,128)(2,1)} %copy-done.11, bf16[256,256]{1,0:T(8,128)(2,1)} %copy-done.9, ...), custom_call_target="tpu_custom_call" | custom-call | flops 1717986944 | bytes 838860 | tf_op jit(solution)/shard_map/sens/pallas_call | solution.py:307
  150.2 0.7 collective-permute-start.29
  151.4 1.4 collective-permute-done.26.came
  153.8 3.1 %pair_sum.7 = (f32[256,256]{1,0:T(8,128)}, bf16[256,256]{1,0:T(8,128)(2,1)}, bf16[256,256]{1,0:T(8,128)(2,1)}, bf16[256,256]{1,0:T(8,128)(2,1)}) custom-call(s32[6]{0:T(128)} %stack.27.pos, bf16[2048,8192]{1,0:T(8,128)(2,1)S(1)} %get-tuple-element.79.slab, f32[1024,256]{1,0:T(8,128)} %get-tuple-element.126.keep, f32[1024,256]{1,0:T(8,128)} %copy-done.5), custom_call_target="tpu_custom_call" | custom-call | flops 104857 | bytes 1048576 | tf_op jit(solution)/shard_map/pair_sum/pallas_call | solution.py:188
  157.3 6.4 %collective-permute-done.28.refs_2_ = bf16[256,256]{1,0:T(8,128)(2,1)S(1)} collective-permute-done((bf16[256,256]{1,0:T(8,128)(2,1)S(1)}, bf16[256,256]{1,0:T(8,128)(2,1)S(1)}, u32[]{:S(2)}, u32[]{:S(2)}) %collective-permute-start.28) | collective-permute-done | bytes 131104 | tf_op jit(solution)/shard_map/ppermute | solution.py:399
  164.3 0.8 collective-permute-done.31.refs_5_
  165.1 1.5 collective-permute-start.46
  167.9 8.0 %sens.8 = bf16[256,4096]{1,0:T(8,128)(2,1)} custom-call(s32[6]{0:T(128)} %stack.27.pos, bf16[2048,8192]{1,0:T(8,128)(2,1)S(1)} %get-tuple-element.79.slab, bf16[256,256]{1,0:T(8,128)(2,1)} %get-tuple-element.130.refs_0_, bf16[256,256]{1,0:T(8,128)(2,1)} %copy-done.19, bf16[256,256]{1,0:T(8,128)(2,1)} %copy-done.18, bf16[256,256]{1,0:T(8,128)(2,1)} %copy-done.17, ...), custom_call_target="tpu_custom_call" | custom-call | flops 1717986944 | bytes 838860 | tf_op jit(solution)/shard_map/sens/pallas_call | solution.py:307
  175.8 1.6 collective-permute-start.47
  177.4 1.4 copy-done.3
  178.8 8.4 %sens.9 = bf16[256,4096]{1,0:T(8,128)(2,1)} custom-call(s32[6]{0:T(128)} %stack.27.pos, bf16[2048,8192]{1,0:T(8,128)(2,1)S(1)} %get-tuple-element.79.slab, bf16[256,256]{1,0:T(8,128)(2,1)} %get-tuple-element.121.refs_0_, bf16[256,256]{1,0:T(8,128)(2,1)} %copy-done.12, bf16[256,256]{1,0:T(8,128)(2,1)} %copy-done.11, bf16[256,256]{1,0:T(8,128)(2,1)} %copy-done.9, ...), custom_call_target="tpu_custom_call" | custom-call | flops 1717986944 | bytes 838860 | tf_op jit(solution)/shard_map/sens/pallas_call | solution.py:307
  187.9 8.4 %sens.10 = bf16[256,4096]{1,0:T(8,128)(2,1)} custom-call(s32[6]{0:T(128)} %stack.27.pos, bf16[2048,8192]{1,0:T(8,128)(2,1)S(1)} %get-tuple-element.79.slab, bf16[256,256]{1,0:T(8,128)(2,1)} %get-tuple-element.130.refs_0_, bf16[256,256]{1,0:T(8,128)(2,1)} %copy-done.19, bf16[256,256]{1,0:T(8,128)(2,1)} %copy-done.18, bf16[256,256]{1,0:T(8,128)(2,1)} %copy-done.17, ...), custom_call_target="tpu_custom_call" | custom-call | flops 1717986944 | bytes 838860 | tf_op jit(solution)/shard_map/sens/pallas_call | solution.py:307
  197.1 6.7 %collective-permute-done.36.refs_0_ = bf16[256,256]{1,0:T(8,128)(2,1)S(1)} collective-permute-done((bf16[256,256]{1,0:T(8,128)(2,1)S(1)}, bf16[256,256]{1,0:T(8,128)(2,1)S(1)}, u32[]{:S(2)}, u32[]{:S(2)}) %collective-permute-start.36) | collective-permute-done | bytes 131104 | tf_op jit(solution)/shard_map/ppermute | solution.py:399
  204.0 7.0 %collective-permute-done.37.refs_1_ = bf16[256,256]{1,0:T(8,128)(2,1)S(1)} collective-permute-done((bf16[256,256]{1,0:T(8,128)(2,1)S(1)}, bf16[256,256]{1,0:T(8,128)(2,1)S(1)}, u32[]{:S(2)}, u32[]{:S(2)}) %collective-permute-start.37) | collective-permute-done | bytes 131104 | tf_op jit(solution)/shard_map/ppermute | solution.py:399
  211.2 4.7 %collective-permute-done.38.refs_2_ = bf16[256,256]{1,0:T(8,128)(2,1)S(1)} collective-permute-done((bf16[256,256]{1,0:T(8,128)(2,1)S(1)}, bf16[256,256]{1,0:T(8,128)(2,1)S(1)}, u32[]{:S(2)}, u32[]{:S(2)}) %collective-permute-start.38) | collective-permute-done | bytes 131104 | tf_op jit(solution)/shard_map/ppermute | solution.py:399
  216.6 3.0 %overload.7 = (f32[256,1024]{1,0:T(8,128)}, bf16[256,256]{1,0:T(8,128)(2,1)}) custom-call(s32[6]{0:T(128)} %stack.27.pos, bf16[2048,8192]{1,0:T(8,128)(2,1)S(1)} %get-tuple-element.79.slab, s32[16,128]{1,0:T(8,128)} %bitcast.10, f32[256,256]{1,0:T(8,128)} %get-tuple-element.139.mine, bf16[256,256]{1,0:T(8,128)(2,1)} %copy-done.45, ...), custom_call_target="tpu_custom_call", output_to_operand_aliasing={{0}: (7, {})} | custom-call | flops 524288 | bytes 419430 | tf_op jit(solution)/shard_map/overload/pallas_call | solution.py:245
  219.7 1.5 collective-permute-done.42.refs_4_
  221.2 2.0 collective-permute-start.41
  223.3 3.7 %collective-permute-done.41.refs_3_ = bf16[256,256]{1,0:T(8,128)(2,1)S(1)} collective-permute-done((bf16[256,256]{1,0:T(8,128)(2,1)}, bf16[256,256]{1,0:T(8,128)(2,1)S(1)}, u32[]{:S(2)}, u32[]{:S(2)}) %collective-permute-start.41) | collective-permute-done | bytes 131104 | tf_op jit(solution)/shard_map/ppermute | solution.py:399
  227.0 0.9 collective-permute-start.40
  227.9 7.8 %collective-permute-done.40.refs_2_ = bf16[256,256]{1,0:T(8,128)(2,1)S(1)} collective-permute-done((bf16[256,256]{1,0:T(8,128)(2,1)}, bf16[256,256]{1,0:T(8,128)(2,1)S(1)}, u32[]{:S(2)}, u32[]{:S(2)}) %collective-permute-start.40) | collective-permute-done | bytes 131104 | tf_op jit(solution)/shard_map/ppermute | solution.py:399
  235.6 7.0 %collective-permute-done.39.refs_1_ = bf16[256,256]{1,0:T(8,128)(2,1)S(1)} collective-permute-done((bf16[256,256]{1,0:T(8,128)(2,1)}, bf16[256,256]{1,0:T(8,128)(2,1)S(1)}, u32[]{:S(2)}, u32[]{:S(2)}) %collective-permute-start.39) | collective-permute-done | bytes 131104 | tf_op jit(solution)/shard_map/ppermute | solution.py:399
  242.6 1.3 collective-permute-done.45.refs_7_
  244.1 1.2 collective-permute-done.44.refs_6_
  245.5 1.2 collective-permute-done.43.refs_5_
  247.3 13.6 %sens.11 = (f32[256,4096]{1,0:T(8,128)}, f32[256,4096]{1,0:T(8,128)}) custom-call(s32[6]{0:T(128)} %stack.27.pos, bf16[2048,8192]{1,0:T(8,128)(2,1)S(1)} %get-tuple-element.79.slab, bf16[256,256]{1,0:T(8,128)(2,1)} %get-tuple-element.146.refs_0_, bf16[256,256]{1,0:T(8,128)(2,1)} %copy-done.35, bf16[256,256]{1,0:T(8,128)(2,1)} %copy-done.32, ...), custom_call_target="tpu_custom_call" | custom-call | flops 3435973888 | bytes 1677721 | tf_op jit(solution)/shard_map/sens/pallas_call | solution.py:307
  261.0 2.2 copy-done
  263.2 3.2 %add_last.2.refs_0_ = f32[8192,256]{1,0:T(8,128)} custom-call(f32[256,4096]{1,0:T(8,128)S(1)} %copy-done, bf16[256,4096]{1,0:T(8,128)(2,1)S(1)} %collective-permute-done.49.came), custom_call_target="tpu_custom_call" | custom-call | flops 419430 | bytes 4194304 | tf_op jit(solution)/shard_map/add_last/pallas_call | solution.py:359
  266.4 2.1 collective-permute-done.48.came
  268.4 3.2 %add_last.3 = f32[8192,256]{1,0:T(8,128)} custom-call(f32[256,4096]{1,0:T(8,128)S(1)} %copy-done.1, bf16[256,4096]{1,0:T(8,128)(2,1)S(1)} %collective-permute-done.48.came, f32[8192,256]{1,0:T(8,128)} %add_last.2.refs_0_), custom_call_target="tpu_custom_call", output_to_operand_aliasing={{}: (2, {})} | custom-call | flops 419430 | bytes 4194304 | tf_op jit(solution)/shard_map/add_last/pallas_call | solution.py:359
  (175 shorter events, 13.6 us)
Async XLA Ops:
  17.4 3.0 %collective-permute-start = (f32[1024,256]{1,0:T(8,128)}, f32[1024,256]{1,0:T(8,128)S(1)}, u32[]{:S(2)}, u32[]{:S(2)}) collective-permute-start(f32[1024,256]{1,0:T(8,128)} %get-tuple-element.81), channel_id=1, source_target_pairs={{0,1},{1,0},{2,3},{3,2},{4,5},{5,4},{6,7},{7,6},{8,9},{9,8},{10,11... | collective-permute-start | bytes 3145736 | tf_op jit(solution)/shard_map/ppermute | solution.py:396
  24.5 20.7 %collective-permute-start.3 = (bf16[256,256]{1,0:T(8,128)(2,1)}, bf16[256,256]{1,0:T(8,128)(2,1)S(1)}, u32[]{:S(2)}, u32[]{:S(2)}) collective-permute-start(bf16[256,256]{1,0:T(8,128)(2,1)} %get-tuple-element.82), channel_id=1, source_target_pairs={{0,6},{1,7},{2,0},{3,1},{4,2},{5,3},{6,4},{7,5},{8,14},{9,15},{10,... | collective-permute-start | bytes 393224 | tf_op jit(solution)/shard_map/ppermute | solution.py:399
  29.5 15.6 %collective-permute-start.1 = (bf16[256,256]{1,0:T(8,128)(2,1)}, bf16[256,256]{1,0:T(8,128)(2,1)S(1)}, u32[]{:S(2)}, u32[]{:S(2)}) collective-permute-start(bf16[256,256]{1,0:T(8,128)(2,1)} %get-tuple-element.87), channel_id=1, source_target_pairs={{0,2},{1,3},{2,4},{3,5},{4,6},{5,7},{6,0},{7,1},{8,10},{9,11},{10,... | collective-permute-start | bytes 393224 | tf_op jit(solution)/shard_map/ppermute | solution.py:399
  29.5 15.6 %collective-permute-start.2 = (bf16[256,256]{1,0:T(8,128)(2,1)}, bf16[256,256]{1,0:T(8,128)(2,1)S(1)}, u32[]{:S(2)}, u32[]{:S(2)}) collective-permute-start(bf16[256,256]{1,0:T(8,128)(2,1)} %get-tuple-element.88), channel_id=1, source_target_pairs={{0,4},{1,5},{2,6},{3,7},{4,0},{5,1},{6,2},{7,3},{8,12},{9,13},{10,... | collective-permute-start | bytes 393224 | tf_op jit(solution)/shard_map/ppermute | solution.py:399
  49.1 5.0 %collective-permute-start.4 = (f32[1024,256]{1,0:T(8,128)S(1)}, f32[1024,256]{1,0:T(8,128)S(1)}, u32[]{:S(2)}, u32[]{:S(2)}) collective-permute-start(f32[1024,256]{1,0:T(8,128)S(1)} %copy-done.52), channel_id=1, source_target_pairs={{0,1},{1,0},{2,3},{3,2},{4,5},{5,4},{6,7},{7,6},{8,9},{9,8},{10,11... | collective-permute-start | bytes 3145736 | tf_op jit(solution)/shard_map/ppermute | solution.py:396
  49.2 23.8 %collective-permute-start.7 = (bf16[256,256]{1,0:T(8,128)(2,1)}, bf16[256,256]{1,0:T(8,128)(2,1)S(1)}, u32[]{:S(2)}, u32[]{:S(2)}) collective-permute-start(bf16[256,256]{1,0:T(8,128)(2,1)} %get-tuple-element.97.refs_0_), channel_id=1, source_target_pairs={{0,6},{1,7},{2,0},{3,1},{4,2},{5,3},{6,4},{7,5},{8,14},{9,15},{10,... | collective-permute-start | bytes 393224 | tf_op jit(solution)/shard_map/ppermute | solution.py:399
  52.0 20.9 %collective-permute-start.6 = (bf16[256,256]{1,0:T(8,128)(2,1)}, bf16[256,256]{1,0:T(8,128)(2,1)S(1)}, u32[]{:S(2)}, u32[]{:S(2)}) collective-permute-start(bf16[256,256]{1,0:T(8,128)(2,1)} %get-tuple-element.97.refs_0_), channel_id=1, source_target_pairs={{0,4},{1,5},{2,6},{3,7},{4,0},{5,1},{6,2},{7,3},{8,12},{9,13},{10,... | collective-permute-start | bytes 393224 | tf_op jit(solution)/shard_map/ppermute | solution.py:399
  54.1 19.0 %collective-permute-start.5 = (bf16[256,256]{1,0:T(8,128)(2,1)}, bf16[256,256]{1,0:T(8,128)(2,1)S(1)}, u32[]{:S(2)}, u32[]{:S(2)}) collective-permute-start(bf16[256,256]{1,0:T(8,128)(2,1)} %get-tuple-element.97.refs_0_), channel_id=1, source_target_pairs={{0,2},{1,3},{2,4},{3,5},{4,6},{5,7},{6,0},{7,1},{8,10},{9,11},{10,... | collective-permute-start | bytes 393224 | tf_op jit(solution)/shard_map/ppermute | solution.py:399
  58.1 14.8 %copy-start.24 = (bf16[256,256]{1,0:T(8,128)(2,1)S(1)}, bf16[256,256]{1,0:T(8,128)(2,1)}, u32[]{:S(2)}) copy-start(bf16[256,256]{1,0:T(8,128)(2,1)} %get-tuple-element.97.refs_0_) | copy-start | bytes 393220
  58.1 15.9 %copy-start.56 = (bf16[256,256]{1,0:T(8,128)(2,1)S(1)}, bf16[256,256]{1,0:T(8,128)(2,1)}, u32[]{:S(2)}) copy-start(bf16[256,256]{1,0:T(8,128)(2,1)} %get-tuple-element.93) | copy-start | bytes 393220
  58.1 19.8 %copy-start.58 = (bf16[256,256]{1,0:T(8,128)(2,1)S(1)}, bf16[256,256]{1,0:T(8,128)(2,1)}, u32[]{:S(2)}) copy-start(bf16[256,256]{1,0:T(8,128)(2,1)} %get-tuple-element.104) | copy-start | bytes 393220
  58.1 19.8 %copy-start.57 = (bf16[256,256]{1,0:T(8,128)(2,1)S(1)}, bf16[256,256]{1,0:T(8,128)(2,1)}, u32[]{:S(2)}) copy-start(bf16[256,256]{1,0:T(8,128)(2,1)} %get-tuple-element.105) | copy-start | bytes 393220
  73.0 4.9 %collective-permute-start.8 = (bf16[256,256]{1,0:T(8,128)(2,1)S(1)}, bf16[256,256]{1,0:T(8,128)(2,1)S(1)}, u32[]{:S(2)}, u32[]{:S(2)}) collective-permute-start(bf16[256,256]{1,0:T(8,128)(2,1)S(1)} %copy-done.24), channel_id=1, source_target_pairs={{0,1},{1,0},{2,3},{3,2},{4,5},{5,4},{6,7},{7,6},{8,9},{9,8},{10,11... | collective-permute-start | bytes 393224 | tf_op jit(solution)/shard_map/ppermute | solution.py:396
  73.1 4.9 %collective-permute-start.9 = (bf16[256,256]{1,0:T(8,128)(2,1)S(1)}, bf16[256,256]{1,0:T(8,128)(2,1)S(1)}, u32[]{:S(2)}, u32[]{:S(2)}) collective-permute-start(bf16[256,256]{1,0:T(8,128)(2,1)S(1)} %collective-permute-done.5.refs_1_), channel_id=1, source_target_pairs={{0,1},{1,0},{2,3},{3,2},{4,5},{5,4},{6,7},{7,6},{8,9},{9,8},{10,11... | collective-permute-start | bytes 393224 | tf_op jit(solution)/shard_map/ppermute | solution.py:396
  73.5 5.3 %collective-permute-start.10 = (bf16[256,256]{1,0:T(8,128)(2,1)S(1)}, bf16[256,256]{1,0:T(8,128)(2,1)S(1)}, u32[]{:S(2)}, u32[]{:S(2)}) collective-permute-start(bf16[256,256]{1,0:T(8,128)(2,1)S(1)} %collective-permute-done.6.refs_2_), channel_id=1, source_target_pairs={{0,1},{1,0},{2,3},{3,2},{4,5},{5,4},{6,7},{7,6},{8,9},{9,8},{10,11... | collective-permute-start | bytes 393224 | tf_op jit(solution)/shard_map/ppermute | solution.py:396
  73.6 5.2 %collective-permute-start.11 = (bf16[256,256]{1,0:T(8,128)(2,1)S(1)}, bf16[256,256]{1,0:T(8,128)(2,1)S(1)}, u32[]{:S(2)}, u32[]{:S(2)}) collective-permute-start(bf16[256,256]{1,0:T(8,128)(2,1)S(1)} %collective-permute-done.7.refs_3_), channel_id=1, source_target_pairs={{0,1},{1,0},{2,3},{3,2},{4,5},{5,4},{6,7},{7,6},{8,9},{9,8},{10,11... | collective-permute-start | bytes 393224 | tf_op jit(solution)/shard_map/ppermute | solution.py:396
  74.1 19.1 %collective-permute-start.14 = (bf16[256,256]{1,0:T(8,128)(2,1)S(1)}, bf16[256,256]{1,0:T(8,128)(2,1)S(1)}, u32[]{:S(2)}, u32[]{:S(2)}) collective-permute-start(bf16[256,256]{1,0:T(8,128)(2,1)S(1)} %copy-done.56), channel_id=1, source_target_pairs={{0,6},{1,7},{2,0},{3,1},{4,2},{5,3},{6,4},{7,5},{8,14},{9,15},{10,... | collective-permute-start | bytes 393224 | tf_op jit(solution)/shard_map/ppermute | solution.py:399
  77.9 15.3 %collective-permute-start.12 = (bf16[256,256]{1,0:T(8,128)(2,1)S(1)}, bf16[256,256]{1,0:T(8,128)(2,1)S(1)}, u32[]{:S(2)}, u32[]{:S(2)}) collective-permute-start(bf16[256,256]{1,0:T(8,128)(2,1)S(1)} %copy-done.58), channel_id=1, source_target_pairs={{0,2},{1,3},{2,4},{3,5},{4,6},{5,7},{6,0},{7,1},{8,10},{9,11},{10,... | collective-permute-start | bytes 393224 | tf_op jit(solution)/shard_map/ppermute | solution.py:399
  78.0 15.2 %collective-permute-start.13 = (bf16[256,256]{1,0:T(8,128)(2,1)S(1)}, bf16[256,256]{1,0:T(8,128)(2,1)S(1)}, u32[]{:S(2)}, u32[]{:S(2)}) collective-permute-start(bf16[256,256]{1,0:T(8,128)(2,1)S(1)} %copy-done.57), channel_id=1, source_target_pairs={{0,4},{1,5},{2,6},{3,7},{4,0},{5,1},{6,2},{7,3},{8,12},{9,13},{10,... | collective-permute-start | bytes 393224 | tf_op jit(solution)/shard_map/ppermute | solution.py:399
  97.1 2.7 %collective-permute-start.15 = (f32[1024,256]{1,0:T(8,128)S(1)}, f32[1024,256]{1,0:T(8,128)S(1)}, u32[]{:S(2)}, u32[]{:S(2)}) collective-permute-start(f32[1024,256]{1,0:T(8,128)S(1)} %copy-done.51), channel_id=1, source_target_pairs={{0,1},{1,0},{2,3},{3,2},{4,5},{5,4},{6,7},{7,6},{8,9},{9,8},{10,11... | collective-permute-start | bytes 3145736 | tf_op jit(solution)/shard_map/ppermute | solution.py:396
  104.1 8.4 %collective-permute-start.16 = (bf16[256,256]{1,0:T(8,128)(2,1)}, bf16[256,256]{1,0:T(8,128)(2,1)S(1)}, u32[]{:S(2)}, u32[]{:S(2)}) collective-permute-start(bf16[256,256]{1,0:T(8,128)(2,1)} %get-tuple-element.116), channel_id=1, source_target_pairs={{0,2},{1,3},{2,4},{3,5},{4,6},{5,7},{6,0},{7,1},{8,10},{9,11},{10,... | collective-permute-start | bytes 393224 | tf_op jit(solution)/shard_map/ppermute | solution.py:399
  107.7 27.3 %collective-permute-start.21 = (bf16[256,256]{1,0:T(8,128)(2,1)S(1)}, bf16[256,256]{1,0:T(8,128)(2,1)S(1)}, u32[]{:S(2)}, u32[]{:S(2)}) collective-permute-start(bf16[256,256]{1,0:T(8,128)(2,1)S(1)} %copy-done.8), channel_id=1, source_target_pairs={{0,6},{1,7},{2,0},{3,1},{4,2},{5,3},{6,4},{7,5},{8,14},{9,15},{10,... | collective-permute-start | bytes 393224 | tf_op jit(solution)/shard_map/ppermute | solution.py:399
  107.9 69.5 %collective-permute-start.35 = (bf16[256,4096]{1,0:T(8,128)(2,1)}, bf16[256,4096]{1,0:T(8,128)(2,1)S(1)}, u32[]{:S(2)}, u32[]{:S(2)}) collective-permute-start(bf16[256,4096]{1,0:T(8,128)(2,1)} %get-tuple-element.101), channel_id=1, source_target_pairs={{0,16},{8,24},{16,0},{24,8},{1,17},{9,25},{17,1},{25,9},{2,18},{10... | collective-permute-start | bytes 6291464 | tf_op jit(solution)/shard_map/ppermute | solution.py:393
  109.5 68.0 %collective-permute-start.34 = (bf16[256,4096]{1,0:T(8,128)(2,1)}, bf16[256,4096]{1,0:T(8,128)(2,1)S(1)}, u32[]{:S(2)}, u32[]{:S(2)}) collective-permute-start(bf16[256,4096]{1,0:T(8,128)(2,1)} %get-tuple-element.135), channel_id=1, source_target_pairs={{0,8},{8,0},{16,24},{24,16},{1,9},{9,1},{17,25},{25,17},{2,10},{10... | collective-permute-start | bytes 6291464 | tf_op jit(solution)/shard_map/ppermute | solution.py:393
  110.9 19.2 %collective-permute-start.18 = (bf16[256,256]{1,0:T(8,128)(2,1)}, bf16[256,256]{1,0:T(8,128)(2,1)S(1)}, u32[]{:S(2)}, u32[]{:S(2)}) collective-permute-start(bf16[256,256]{1,0:T(8,128)(2,1)} %get-tuple-element.111), channel_id=1, source_target_pairs={{0,6},{1,7},{2,0},{3,1},{4,2},{5,3},{6,4},{7,5},{8,14},{9,15},{10,... | collective-permute-start | bytes 393224 | tf_op jit(solution)/shard_map/ppermute | solution.py:399
  112.5 16.4 %copy-start.30 = (bf16[256,256]{1,0:T(8,128)(2,1)}, bf16[256,256]{1,0:T(8,128)(2,1)S(1)}, u32[]{:S(2)}) copy-start(bf16[256,256]{1,0:T(8,128)(2,1)S(1)} %collective-permute-done.16.refs_0_) | copy-start | bytes 393220
  112.5 16.4 %collective-permute-start.17 = (bf16[256,256]{1,0:T(8,128)(2,1)}, bf16[256,256]{1,0:T(8,128)(2,1)S(1)}, u32[]{:S(2)}, u32[]{:S(2)}) collective-permute-start(bf16[256,256]{1,0:T(8,128)(2,1)} %get-tuple-element.117), channel_id=1, source_target_pairs={{0,4},{1,5},{2,6},{3,7},{4,0},{5,1},{6,2},{7,3},{8,12},{9,13},{10,... | collective-permute-start | bytes 393224 | tf_op jit(solution)/shard_map/ppermute | solution.py:399
  128.9 10.2 %collective-permute-start.20 = (bf16[256,256]{1,0:T(8,128)(2,1)S(1)}, bf16[256,256]{1,0:T(8,128)(2,1)S(1)}, u32[]{:S(2)}, u32[]{:S(2)}) collective-permute-start(bf16[256,256]{1,0:T(8,128)(2,1)S(1)} %copy-done.8), channel_id=1, source_target_pairs={{0,4},{1,5},{2,6},{3,7},{4,0},{5,1},{6,2},{7,3},{8,12},{9,13},{10,... | collective-permute-start | bytes 393224 | tf_op jit(solution)/shard_map/ppermute | solution.py:399
  130.1 8.9 %collective-permute-start.19 = (bf16[256,256]{1,0:T(8,128)(2,1)S(1)}, bf16[256,256]{1,0:T(8,128)(2,1)S(1)}, u32[]{:S(2)}, u32[]{:S(2)}) collective-permute-start(bf16[256,256]{1,0:T(8,128)(2,1)S(1)} %copy-done.8), channel_id=1, source_target_pairs={{0,2},{1,3},{2,4},{3,5},{4,6},{5,7},{6,0},{7,1},{8,10},{9,11},{10,... | collective-permute-start | bytes 393224 | tf_op jit(solution)/shard_map/ppermute | solution.py:399
  134.9 15.3 %copy-start.10 = (bf16[256,256]{1,0:T(8,128)(2,1)S(1)}, bf16[256,256]{1,0:T(8,128)(2,1)}, u32[]{:S(2)}) copy-start(bf16[256,256]{1,0:T(8,128)(2,1)} %get-tuple-element.130.refs_0_) | copy-start | bytes 393220
  135.0 4.7 %collective-permute-start.22 = (bf16[256,256]{1,0:T(8,128)(2,1)S(1)}, bf16[256,256]{1,0:T(8,128)(2,1)S(1)}, u32[]{:S(2)}, u32[]{:S(2)}) collective-permute-start(bf16[256,256]{1,0:T(8,128)(2,1)S(1)} %copy-done.8), channel_id=1, source_target_pairs={{0,1},{1,0},{2,3},{3,2},{4,5},{5,4},{6,7},{7,6},{8,9},{9,8},{10,11... | collective-permute-start | bytes 393224 | tf_op jit(solution)/shard_map/ppermute | solution.py:396
  139.1 1.4 collective-permute-start.23
  139.2 1.5 collective-permute-start.24
  139.7 1.3 collective-permute-start.25
  149.9 2.9 %collective-permute-start.26 = (f32[1024,256]{1,0:T(8,128)}, f32[1024,256]{1,0:T(8,128)S(1)}, u32[]{:S(2)}, u32[]{:S(2)}) collective-permute-start(f32[1024,256]{1,0:T(8,128)} %get-tuple-element.127), channel_id=1, source_target_pairs={{0,1},{1,0},{2,3},{3,2},{4,5},{5,4},{6,7},{7,6},{8,9},{9,8},{10,11... | collective-permute-start | bytes 3145736 | tf_op jit(solution)/shard_map/ppermute | solution.py:396
  150.2 6.6 %collective-permute-start.29 = (bf16[256,256]{1,0:T(8,128)(2,1)S(1)}, bf16[256,256]{1,0:T(8,128)(2,1)S(1)}, u32[]{:S(2)}, u32[]{:S(2)}) collective-permute-start(bf16[256,256]{1,0:T(8,128)(2,1)S(1)} %copy-done.10), channel_id=1, source_target_pairs={{0,6},{1,7},{2,0},{3,1},{4,2},{5,3},{6,4},{7,5},{8,14},{9,15},{10,... | collective-permute-start | bytes 393224 | tf_op jit(solution)/shard_map/ppermute | solution.py:399
  151.0 12.7 %collective-permute-start.28 = (bf16[256,256]{1,0:T(8,128)(2,1)S(1)}, bf16[256,256]{1,0:T(8,128)(2,1)S(1)}, u32[]{:S(2)}, u32[]{:S(2)}) collective-permute-start(bf16[256,256]{1,0:T(8,128)(2,1)S(1)} %copy-done.10), channel_id=1, source_target_pairs={{0,4},{1,5},{2,6},{3,7},{4,0},{5,1},{6,2},{7,3},{8,12},{9,13},{10,... | collective-permute-start | bytes 393224 | tf_op jit(solution)/shard_map/ppermute | solution.py:399
  152.8 10.9 %collective-permute-start.27 = (bf16[256,256]{1,0:T(8,128)(2,1)S(1)}, bf16[256,256]{1,0:T(8,128)(2,1)S(1)}, u32[]{:S(2)}, u32[]{:S(2)}) collective-permute-start(bf16[256,256]{1,0:T(8,128)(2,1)S(1)} %copy-done.10), channel_id=1, source_target_pairs={{0,2},{1,3},{2,4},{3,5},{4,6},{5,7},{6,0},{7,1},{8,10},{9,11},{10,... | collective-permute-start | bytes 393224 | tf_op jit(solution)/shard_map/ppermute | solution.py:399
  156.9 9.7 %copy-start.17 = (bf16[256,256]{1,0:T(8,128)(2,1)}, bf16[256,256]{1,0:T(8,128)(2,1)S(1)}, u32[]{:S(2)}) copy-start(bf16[256,256]{1,0:T(8,128)(2,1)S(1)} %collective-permute-done.29.refs_3_) | copy-start | bytes 393220
  156.9 7.4 %collective-permute-start.30 = (bf16[256,256]{1,0:T(8,128)(2,1)S(1)}, bf16[256,256]{1,0:T(8,128)(2,1)S(1)}, u32[]{:S(2)}, u32[]{:S(2)}) collective-permute-start(bf16[256,256]{1,0:T(8,128)(2,1)S(1)} %copy-done.10), channel_id=1, source_target_pairs={{0,1},{1,0},{2,3},{3,2},{4,5},{5,4},{6,7},{7,6},{8,9},{9,8},{10,11... | collective-permute-start | bytes 393224 | tf_op jit(solution)/shard_map/ppermute | solution.py:396
  163.7 1.4 collective-permute-start.31
  163.7 2.8 %collective-permute-start.32 = (bf16[256,256]{1,0:T(8,128)(2,1)S(1)}, bf16[256,256]{1,0:T(8,128)(2,1)S(1)}, u32[]{:S(2)}, u32[]{:S(2)}) collective-permute-start(bf16[256,256]{1,0:T(8,128)(2,1)S(1)} %collective-permute-done.28.refs_2_), channel_id=1, source_target_pairs={{0,1},{1,0},{2,3},{3,2},{4,5},{5,4},{6,7},{7,6},{8,9},{9,8},{10,11... | collective-permute-start | bytes 393224 | tf_op jit(solution)/shard_map/ppermute | solution.py:396
  164.2 2.3 collective-permute-start.33
  165.1 81.6 %collective-permute-start.46 = (bf16[256,4096]{1,0:T(8,128)(2,1)}, bf16[256,4096]{1,0:T(8,128)(2,1)}, u32[]{:S(2)}, u32[]{:S(2)}) collective-permute-start(bf16[256,4096]{1,0:T(8,128)(2,1)} %sens.7), channel_id=1, source_target_pairs={{0,8},{8,0},{16,24},{24,16},{1,9},{9,1},{17,25},{25,17},{2,10},{10... | collective-permute-start | bytes 6291464 | tf_op jit(solution)/shard_map/ppermute | solution.py:393
  175.8 70.9 %collective-permute-start.47 = (bf16[256,4096]{1,0:T(8,128)(2,1)}, bf16[256,4096]{1,0:T(8,128)(2,1)}, u32[]{:S(2)}, u32[]{:S(2)}) collective-permute-start(bf16[256,4096]{1,0:T(8,128)(2,1)} %sens.8), channel_id=1, source_target_pairs={{0,16},{8,24},{16,0},{24,8},{1,17},{9,25},{17,1},{25,9},{2,18},{10... | collective-permute-start | bytes 6291464 | tf_op jit(solution)/shard_map/ppermute | solution.py:393
  177.4 9.8 %copy-start.2 = (bf16[256,4096]{1,0:T(8,128)(2,1)}, bf16[256,4096]{1,0:T(8,128)(2,1)S(1)}, u32[]{:S(2)}) copy-start(bf16[256,4096]{1,0:T(8,128)(2,1)S(1)} %collective-permute-done.34.refs_8_) | copy-start | bytes 6291460
  187.2 16.6 %copy-start.54 = (bf16[256,256]{1,0:T(8,128)(2,1)S(1)}, bf16[256,256]{1,0:T(8,128)(2,1)}, u32[]{:S(2)}) copy-start(bf16[256,256]{1,0:T(8,128)(2,1)} %get-tuple-element.141) | copy-start | bytes 393220
  187.2 23.7 %copy-start.53 = (bf16[256,256]{1,0:T(8,128)(2,1)S(1)}, bf16[256,256]{1,0:T(8,128)(2,1)}, u32[]{:S(2)}) copy-start(bf16[256,256]{1,0:T(8,128)(2,1)} %get-tuple-element.128) | copy-start | bytes 393220
  187.3 73.7 %collective-permute-start.49 = (bf16[256,4096]{1,0:T(8,128)(2,1)}, bf16[256,4096]{1,0:T(8,128)(2,1)S(1)}, u32[]{:S(2)}, u32[]{:S(2)}) collective-permute-start(bf16[256,4096]{1,0:T(8,128)(2,1)} %sens.9), channel_id=1, source_target_pairs={{0,8},{8,0},{16,24},{24,16},{1,9},{9,1},{17,25},{25,17},{2,10},{10... | collective-permute-start | bytes 6291464 | tf_op jit(solution)/shard_map/ppermute | solution.py:393
  196.3 72.1 %collective-permute-start.48 = (bf16[256,4096]{1,0:T(8,128)(2,1)}, bf16[256,4096]{1,0:T(8,128)(2,1)S(1)}, u32[]{:S(2)}, u32[]{:S(2)}) collective-permute-start(bf16[256,4096]{1,0:T(8,128)(2,1)} %sens.10), channel_id=1, source_target_pairs={{0,16},{8,24},{16,0},{24,8},{1,17},{9,25},{17,1},{25,9},{2,18},{10... | collective-permute-start | bytes 6291464 | tf_op jit(solution)/shard_map/ppermute | solution.py:393
  196.9 6.9 %collective-permute-start.36 = (bf16[256,256]{1,0:T(8,128)(2,1)S(1)}, bf16[256,256]{1,0:T(8,128)(2,1)S(1)}, u32[]{:S(2)}, u32[]{:S(2)}) collective-permute-start(bf16[256,256]{1,0:T(8,128)(2,1)S(1)} %copy-done.55), channel_id=1, source_target_pairs={{0,2},{1,3},{2,4},{3,5},{4,6},{5,7},{6,0},{7,1},{8,10},{9,11},{10,... | collective-permute-start | bytes 393224 | tf_op jit(solution)/shard_map/ppermute | solution.py:399
  203.8 12.1 %copy-start.45 = (bf16[256,256]{1,0:T(8,128)(2,1)}, bf16[256,256]{1,0:T(8,128)(2,1)S(1)}, u32[]{:S(2)}) copy-start(bf16[256,256]{1,0:T(8,128)(2,1)S(1)} %collective-permute-done.36.refs_0_) | copy-start | bytes 393220
  203.8 7.1 %collective-permute-start.37 = (bf16[256,256]{1,0:T(8,128)(2,1)S(1)}, bf16[256,256]{1,0:T(8,128)(2,1)S(1)}, u32[]{:S(2)}, u32[]{:S(2)}) collective-permute-start(bf16[256,256]{1,0:T(8,128)(2,1)S(1)} %copy-done.54), channel_id=1, source_target_pairs={{0,4},{1,5},{2,6},{3,7},{4,0},{5,1},{6,2},{7,3},{8,12},{9,13},{10,... | collective-permute-start | bytes 393224 | tf_op jit(solution)/shard_map/ppermute | solution.py:399
  211.0 5.0 %collective-permute-start.38 = (bf16[256,256]{1,0:T(8,128)(2,1)S(1)}, bf16[256,256]{1,0:T(8,128)(2,1)S(1)}, u32[]{:S(2)}, u32[]{:S(2)}) collective-permute-start(bf16[256,256]{1,0:T(8,128)(2,1)S(1)} %copy-done.53), channel_id=1, source_target_pairs={{0,6},{1,7},{2,0},{3,1},{4,2},{5,3},{6,4},{7,5},{8,14},{9,15},{10,... | collective-permute-start | bytes 393224 | tf_op jit(solution)/shard_map/ppermute | solution.py:399
  219.6 1.6 collective-permute-start.42
  221.2 25.5 %copy-start.28 = (bf16[256,256]{1,0:T(8,128)(2,1)}, bf16[256,256]{1,0:T(8,128)(2,1)S(1)}, u32[]{:S(2)}) copy-start(bf16[256,256]{1,0:T(8,128)(2,1)S(1)} %collective-permute-done.42.refs_4_) | copy-start | bytes 393220
  221.2 5.8 %collective-permute-start.41 = (bf16[256,256]{1,0:T(8,128)(2,1)}, bf16[256,256]{1,0:T(8,128)(2,1)S(1)}, u32[]{:S(2)}, u32[]{:S(2)}) collective-permute-start(bf16[256,256]{1,0:T(8,128)(2,1)} %get-tuple-element.146.refs_0_), channel_id=1, source_target_pairs={{0,6},{1,7},{2,0},{3,1},{4,2},{5,3},{6,4},{7,5},{8,14},{9,15},{10,... | collective-permute-start | bytes 393224 | tf_op jit(solution)/shard_map/ppermute | solution.py:399
  227.0 19.7 %copy-start.29 = (bf16[256,256]{1,0:T(8,128)(2,1)}, bf16[256,256]{1,0:T(8,128)(2,1)S(1)}, u32[]{:S(2)}) copy-start(bf16[256,256]{1,0:T(8,128)(2,1)S(1)} %collective-permute-done.41.refs_3_) | copy-start | bytes 393220
  227.0 8.6 %collective-permute-start.40 = (bf16[256,256]{1,0:T(8,128)(2,1)}, bf16[256,256]{1,0:T(8,128)(2,1)S(1)}, u32[]{:S(2)}, u32[]{:S(2)}) collective-permute-start(bf16[256,256]{1,0:T(8,128)(2,1)} %get-tuple-element.146.refs_0_), channel_id=1, source_target_pairs={{0,4},{1,5},{2,6},{3,7},{4,0},{5,1},{6,2},{7,3},{8,12},{9,13},{10,... | collective-permute-start | bytes 393224 | tf_op jit(solution)/shard_map/ppermute | solution.py:399
  235.6 11.1 %copy-start.32 = (bf16[256,256]{1,0:T(8,128)(2,1)}, bf16[256,256]{1,0:T(8,128)(2,1)S(1)}, u32[]{:S(2)}) copy-start(bf16[256,256]{1,0:T(8,128)(2,1)S(1)} %collective-permute-done.40.refs_2_) | copy-start | bytes 393220
  235.6 7.0 %collective-permute-start.39 = (bf16[256,256]{1,0:T(8,128)(2,1)}, bf16[256,256]{1,0:T(8,128)(2,1)S(1)}, u32[]{:S(2)}, u32[]{:S(2)}) collective-permute-start(bf16[256,256]{1,0:T(8,128)(2,1)} %get-tuple-element.146.refs_0_), channel_id=1, source_target_pairs={{0,2},{1,3},{2,4},{3,5},{4,6},{5,7},{6,0},{7,1},{8,10},{9,11},{10,... | collective-permute-start | bytes 393224 | tf_op jit(solution)/shard_map/ppermute | solution.py:399
  242.6 1.3 collective-permute-start.45
  244.0 1.3 collective-permute-start.44
  245.3 1.3 collective-permute-start.43
  (45 other events, 104.3 us)

commit v3 on v2

--- a/solution.py
+++ b/solution.py
@@ -432,20 +432,25 @@
     adj_far = adjoints(flow_far, far)
     flow_over = pair(*over_parts)
     up_parts = flows(up)
-    far_a, far_b = sens(shared(adj_far), (0, 1))
+    adj_far = shared(adj_far)
+    arrived(*flow_over[1])
+    far_a, far_b = sens(adj_far, (0, 1))
     far_a, far_b = across(far_a, 1), across(far_b, 2)
     adj_over = adjoints(flow_over, over)
     flow_up = pair(*up_parts)
     home_parts = flows(home)
+    arrived(*adj_over)
     adj_up = adjoints(flow_up, up)
     adj_over = shared(adj_over)
-    over_a = across(sens(adj_over, (0,))[0], 1)
+    (over_a,) = sens(adj_over, (0,))
+    adj_up = shared(adj_up)
+    arrived(far_a, far_b)
+    (up_b,) = sens(adj_up, (1,))
+    over_a, up_b = across(gate(over_a), 1), across(up_b, 2)
     flow_home = pair(*home_parts)
-    adj_up = shared(adj_up)
-    up_b = across(sens(adj_up, (1,))[0], 2)
-    arrived(far_a, far_b)
     over_b = across(sens(adj_over, (1,), adds=(far_b,))[0], 1)
     up_a = across(sens(adj_up, (0,), adds=(far_a,))[0], 2)
+    arrived(over_a, up_b)
     adj_home = adjoints(flow_home, home)
     total_a, total_b = sens(shared(adj_home), (0, 1), adds=(over_a, up_b), dtype=F32)
     total = add_last(total_b, over_b, 1, None)

time: 272 us -> 270 us (level)
  waiting for transfers between devices: 63.6 us -> 58.9 us
  starting transfers between devices: 42.3 us -> 46.4 us
    ppermute x6, waiting for transfers between devices: 2.08 us -> 23.4 us  [across(): return lax.ppermute(x, 'br', [(i, i ^ bit) for i in range(4)])]
    ppermute x24, waiting for transfers between devices: 47.7 us -> 27.2 us  [chip_ahead(): return lax.ppermute(x, 'bus', [(i, (i + 2 * k) % 8) for i in range(8)])]
    ppermute x20, waiting for transfers between devices: 13.9 us -> 8.25 us  [swap(): return lax.ppermute(x, 'bus', [(i, i ^ 1) for i in range(8)])]
    ppermute x24, starting transfers between devices: 30.8 us -> 35.9 us  [chip_ahead(): return lax.ppermute(x, 'bus', [(i, (i + 2 * k) % 8) for i in range(8)])]
    unnamed x118 -> x112, local copies, waits for them, and re-layouts: 13.1 us -> 12 us
  transfers between devices with their start and end apart: 50 -> 50, of which waited for: 21 -> 20; matrix products, arithmetic and copies ran while one was open for 0% -> 0% of each run, Pallas kernels for 44% -> 39%
where the time goes in v3:
time: 270 us
  Pallas kernels  150 us (56%)
  waiting for transfers between devices  58.9 us (22%)
  starting transfers between devices  46.4 us (17%)
  local copies, waits for them, and re-layouts  12.6 us (5%)
    pallas_call x4, Pallas kernels, partial_flows(): call(functools.partial(flows_kernel, first, bounds, depth, block), 'flows...  59.9 us
    pallas_call x6, Pallas kernels, partial_sens(): call(functools.partial(sens_kernel, halves, block, len(adds)), 'sens', [j...  59.3 us
    ppermute x24, starting transfers between devices, chip_ahead(): return lax.ppermute(x, 'bus', [(i, (i + 2 * k) % 8) for i in range(8)])  35.9 us
    ppermute x24, waiting for transfers between devices, chip_ahead(): return lax.ppermute(x, 'bus', [(i, (i + 2 * k) % 8) for i in range(8)])  27.2 us
    ppermute x6, waiting for transfers between devices, across(): return lax.ppermute(x, 'br', [(i, i ^ bit) for i in range(4)])  23.4 us
    pallas_call x4, Pallas kernels, overload(): call(functools.partial(overload_kernel, len(came), block, parts, part), '...  12.3 us
    pallas_call x4, Pallas kernels, pair_sum(): call(pair_kernel, 'pair_sum', [jax.ShapeDtypeStruct((own, hours), F32)] +...  12.2 us
    unnamed x112, local copies, waits for them, and re-layouts  12 us
  transfers between devices with their start and end apart: 50, of which 20 were waited for; matrix products, arithmetic and copies ran while one was open for 0% of the time, Pallas kernels for 39%

profile of v3, /device:TPU:0, one launch (start us, length us, event | category | flops | bytes accessed | tf_op | source)
XLA Modules:
  0.0 269.5 jit_solution(7914199735664002753)
XLA Ops:
  0.6 0.6 stack.27.pos
  1.2 16.1 %flows.4 = (bf16[2048,8192]{1,0:T(8,128)(2,1)S(1)}, f32[1024,256]{1,0:T(8,128)}, f32[1024,256]{1,0:T(8,128)}) custom-call(s32[6]{0:T(128)} %stack.27.pos, bf16[2048,8192]{1,0:T(8,128)(2,1)} %slab.1, s32[8192,1024]{1,0:T(8,128)} %codes.7), custom_call_target="tpu_custom_call" | custom-call | flops 3435973888 | bytes 13421772 | tf_op jit(solution)/shard_map/flows/pallas_call | solution.py:150
  17.9 2.5 collective-permute-done.came
  20.4 1.0 copy-done.7
  21.4 3.1 %pair_sum.4 = (f32[256,256]{1,0:T(8,128)}, bf16[256,256]{1,0:T(8,128)(2,1)}, bf16[256,256]{1,0:T(8,128)(2,1)}, bf16[256,256]{1,0:T(8,128)(2,1)}) custom-call(s32[6]{0:T(128)} %stack.27.pos, bf16[2048,8192]{1,0:T(8,128)(2,1)S(1)} %get-tuple-element.83.slab, f32[1024,256]{1,0:T(8,128)} %get-tuple-element.84.keep, f32[1024,256]{1,0:T(8,128)} %copy-done.7), custom_call_target="tpu_custom_call" | custom-call | flops 104857 | bytes 1048576 | tf_op jit(solution)/shard_map/pair_sum/pallas_call | solution.py:188
  24.4 5.0 %collective-permute-start.3 = (bf16[256,256]{1,0:T(8,128)(2,1)}, bf16[256,256]{1,0:T(8,128)(2,1)S(1)}, u32[]{:S(2)}, u32[]{:S(2)}) collective-permute-start(bf16[256,256]{1,0:T(8,128)(2,1)} %get-tuple-element.86), channel_id=1, source_target_pairs={{0,6},{1,7},{2,0},{3,1},{4,2},{5,3},{6,4},{7,5},{8,14},{9,15},{10,... | collective-permute-start | bytes 393224 | tf_op jit(solution)/shard_map/ppermute | solution.py:399
  29.4 1.0 collective-permute-start.2
  30.5 14.6 %flows.5 = (f32[1024,256]{1,0:T(8,128)}, f32[1024,256]{1,0:T(8,128)}) custom-call(s32[6]{0:T(128)} %stack.27.pos, bf16[2048,8192]{1,0:T(8,128)(2,1)S(1)} %get-tuple-element.83.slab, s32[8192,1024]{1,0:T(8,128)} %codes.7), custom_call_target="tpu_custom_call" | custom-call | flops 3435973888 | bytes 3355443 | tf_op jit(solution)/shard_map/flows/pallas_call | solution.py:150
  45.1 0.6 copy-done.46
  45.9 3.2 %overload.4 = (f32[256,1024]{1,0:T(8,128)}, bf16[256,256]{1,0:T(8,128)(2,1)}) custom-call(s32[6]{0:T(128)} %stack.27.pos, bf16[2048,8192]{1,0:T(8,128)(2,1)S(1)} %get-tuple-element.83.slab, s32[16,128]{1,0:T(8,128)} %bitcast.7, f32[256,256]{1,0:T(8,128)} %get-tuple-element.90.mine, bf16[256,256]{1,0:T(8,128)(2,1)} %copy-done.46, ...), custom_call_target="tpu_custom_call" | custom-call | flops 524288 | bytes 419430 | tf_op jit(solution)/shard_map/overload/pallas_call | solution.py:245
  49.1 2.9 %collective-permute-start.10 = (bf16[256,256]{1,0:T(8,128)(2,1)}, bf16[256,256]{1,0:T(8,128)(2,1)S(1)}, u32[]{:S(2)}, u32[]{:S(2)}) collective-permute-start(bf16[256,256]{1,0:T(8,128)(2,1)} %get-tuple-element.104.refs_0_), channel_id=1, source_target_pairs={{0,6},{1,7},{2,0},{3,1},{4,2},{5,3},{6,4},{7,5},{8,14},{9,15},{10,... | collective-permute-start | bytes 393224 | tf_op jit(solution)/shard_map/ppermute | solution.py:399
  52.0 2.0 collective-permute-start.9
  54.0 1.0 copy-done.4
  55.0 3.1 %pair_sum.5 = (f32[256,256]{1,0:T(8,128)}, bf16[256,256]{1,0:T(8,128)(2,1)}, bf16[256,256]{1,0:T(8,128)(2,1)}, bf16[256,256]{1,0:T(8,128)(2,1)}) custom-call(s32[6]{0:T(128)} %stack.27.pos, bf16[2048,8192]{1,0:T(8,128)(2,1)S(1)} %get-tuple-element.83.slab, f32[1024,256]{1,0:T(8,128)} %get-tuple-element.95.keep, f32[1024,256]{1,0:T(8,128)} %copy-done.4), custom_call_target="tpu_custom_call" | custom-call | flops 104857 | bytes 1048576 | tf_op jit(solution)/shard_map/pair_sum/pallas_call | solution.py:188
  58.0 1.5 collective-permute-start.5
  59.5 2.9 %collective-permute-start.6 = (bf16[256,256]{1,0:T(8,128)(2,1)}, bf16[256,256]{1,0:T(8,128)(2,1)S(1)}, u32[]{:S(2)}, u32[]{:S(2)}) collective-permute-start(bf16[256,256]{1,0:T(8,128)(2,1)} %get-tuple-element.102), channel_id=1, source_target_pairs={{0,4},{1,5},{2,6},{3,7},{4,0},{5,1},{6,2},{7,3},{8,12},{9,13},{10,... | collective-permute-start | bytes 393224 | tf_op jit(solution)/shard_map/ppermute | solution.py:399
  62.5 14.6 %flows.6 = (f32[1024,256]{1,0:T(8,128)}, f32[1024,256]{1,0:T(8,128)}) custom-call(s32[6]{0:T(128)} %stack.27.pos, bf16[2048,8192]{1,0:T(8,128)(2,1)S(1)} %get-tuple-element.83.slab, s32[8192,1024]{1,0:T(8,128)} %codes.7), custom_call_target="tpu_custom_call" | custom-call | flops 3435973888 | bytes 3355443 | tf_op jit(solution)/shard_map/flows/pallas_call | solution.py:150
  78.4 3.7 %collective-permute-done.7.refs_2_ = bf16[256,256]{1,0:T(8,128)(2,1)S(1)} collective-permute-done((bf16[256,256]{1,0:T(8,128)(2,1)S(1)}, bf16[256,256]{1,0:T(8,128)(2,1)S(1)}, u32[]{:S(2)}, u32[]{:S(2)}) %collective-permute-start.7) | collective-permute-done | bytes 131104 | tf_op jit(solution)/shard_map/ppermute | solution.py:399
  82.2 0.6 copy-done.34
  83.0 0.6 copy-done.45
  83.6 13.0 %sens.6 = (bf16[256,4096]{1,0:T(8,128)(2,1)}, bf16[256,4096]{1,0:T(8,128)(2,1)}) custom-call(s32[6]{0:T(128)} %stack.27.pos, bf16[2048,8192]{1,0:T(8,128)(2,1)S(1)} %get-tuple-element.83.slab, bf16[256,256]{1,0:T(8,128)(2,1)} %get-tuple-element.104.refs_0_, bf16[256,256]{1,0:T(8,128)(2,1)} %copy-done.29, bf16[256,256]{1,0:T(8,128)(2,1)} %copy-done.27, ...), custom_call_target="tpu_custom_call" | custom-call | flops 3435973888 | bytes 1677721 | tf_op jit(solution)/shard_map/sens/pallas_call | solution.py:307
  96.6 1.6 collective-permute-start.26
  98.2 1.5 collective-permute-start.27
  99.7 3.0 %overload.5 = (f32[256,1024]{1,0:T(8,128)}, bf16[256,256]{1,0:T(8,128)(2,1)}) custom-call(s32[6]{0:T(128)} %stack.27.pos, bf16[2048,8192]{1,0:T(8,128)(2,1)S(1)} %get-tuple-element.83.slab, s32[16,128]{1,0:T(8,128)} %bitcast.8, f32[256,256]{1,0:T(8,128)} %get-tuple-element.110.mine, bf16[256,256]{1,0:T(8,128)(2,1)} %copy-done.26, ...), custom_call_target="tpu_custom_call", output_to_operand_aliasing={{0}: (7, {})} | custom-call | flops 524288 | bytes 419430 | tf_op jit(solution)/shard_map/overload/pallas_call | solution.py:245
  102.8 1.9 collective-permute-start.18
  104.7 0.9 collective-permute-done.15.came
  105.7 0.9 copy-done.5
  106.6 3.1 %pair_sum.6 = (f32[256,256]{1,0:T(8,128)}, bf16[256,256]{1,0:T(8,128)(2,1)}, bf16[256,256]{1,0:T(8,128)(2,1)}, bf16[256,256]{1,0:T(8,128)(2,1)}) custom-call(s32[6]{0:T(128)} %stack.27.pos, bf16[2048,8192]{1,0:T(8,128)(2,1)S(1)} %get-tuple-element.83.slab, f32[1024,256]{1,0:T(8,128)} %get-tuple-element.114.keep, f32[1024,256]{1,0:T(8,128)} %copy-done.5), custom_call_target="tpu_custom_call" | custom-call | flops 104857 | bytes 1048576 | tf_op jit(solution)/shard_map/pair_sum/pallas_call | solution.py:188
  109.7 3.5 %collective-permute-start.21 = (bf16[256,256]{1,0:T(8,128)(2,1)}, bf16[256,256]{1,0:T(8,128)(2,1)S(1)}, u32[]{:S(2)}, u32[]{:S(2)}) collective-permute-start(bf16[256,256]{1,0:T(8,128)(2,1)} %get-tuple-element.116), channel_id=1, source_target_pairs={{0,6},{1,7},{2,0},{3,1},{4,2},{5,3},{6,4},{7,5},{8,14},{9,15},{10,... | collective-permute-start | bytes 393224 | tf_op jit(solution)/shard_map/ppermute | solution.py:399
  113.2 4.4 %collective-permute-done.17.refs_2_ = bf16[256,256]{1,0:T(8,128)(2,1)S(1)} collective-permute-done((bf16[256,256]{1,0:T(8,128)(2,1)}, bf16[256,256]{1,0:T(8,128)(2,1)S(1)}, u32[]{:S(2)}, u32[]{:S(2)}) %collective-permute-start.17) | collective-permute-done | bytes 131104 | tf_op jit(solution)/shard_map/ppermute | solution.py:399
  117.6 5.0 %collective-permute-start.20 = (bf16[256,256]{1,0:T(8,128)(2,1)}, bf16[256,256]{1,0:T(8,128)(2,1)S(1)}, u32[]{:S(2)}, u32[]{:S(2)}) collective-permute-start(bf16[256,256]{1,0:T(8,128)(2,1)} %get-tuple-element.123), channel_id=1, source_target_pairs={{0,4},{1,5},{2,6},{3,7},{4,0},{5,1},{6,2},{7,3},{8,12},{9,13},{10,... | collective-permute-start | bytes 393224 | tf_op jit(solution)/shard_map/ppermute | solution.py:399
  122.6 14.6 %flows.7 = (f32[1024,256]{1,0:T(8,128)}, f32[1024,256]{1,0:T(8,128)}) custom-call(s32[6]{0:T(128)} %stack.27.pos, bf16[2048,8192]{1,0:T(8,128)(2,1)S(1)} %get-tuple-element.83.slab, s32[8192,1024]{1,0:T(8,128)} %codes.7), custom_call_target="tpu_custom_call" | custom-call | flops 3435973888 | bytes 3355443 | tf_op jit(solution)/shard_map/flows/pallas_call | solution.py:150
  137.3 0.6 copy-done.41
  138.0 3.2 %overload.6 = (f32[256,1024]{1,0:T(8,128)}, bf16[256,256]{1,0:T(8,128)(2,1)}) custom-call(s32[6]{0:T(128)} %stack.27.pos, bf16[2048,8192]{1,0:T(8,128)(2,1)S(1)} %get-tuple-element.83.slab, s32[16,128]{1,0:T(8,128)} %bitcast.9, f32[256,256]{1,0:T(8,128)} %get-tuple-element.121.mine, bf16[256,256]{1,0:T(8,128)(2,1)} %copy-done.41, ...), custom_call_target="tpu_custom_call", output_to_operand_aliasing={{0}: (7, {})} | custom-call | flops 524288 | bytes 419430 | tf_op jit(solution)/shard_map/overload/pallas_call | solution.py:245
  141.8 0.7 collective-permute-done.22.refs_4_
  142.8 0.6 collective-permute-start.30
  143.9 0.9 collective-permute-start.28
  144.9 7.9 %sens.7 = bf16[256,4096]{1,0:T(8,128)(2,1)} custom-call(s32[6]{0:T(128)} %stack.27.pos, bf16[2048,8192]{1,0:T(8,128)(2,1)S(1)} %get-tuple-element.83.slab, bf16[256,256]{1,0:T(8,128)(2,1)} %get-tuple-element.127.refs_0_, bf16[256,256]{1,0:T(8,128)(2,1)} %copy-done.11, bf16[256,256]{1,0:T(8,128)(2,1)} %copy-done.10, bf16[256,256]{1,0:T(8,128)(2,1)} %copy-done.9, ...), custom_call_target="tpu_custom_call" | custom-call | flops 1717986944 | bytes 838860 | tf_op jit(solution)/shard_map/sens/pallas_call | solution.py:307
  152.8 3.1 %collective-permute-done.29.refs_2_ = bf16[256,256]{1,0:T(8,128)(2,1)S(1)} collective-permute-done((bf16[256,256]{1,0:T(8,128)(2,1)}, bf16[256,256]{1,0:T(8,128)(2,1)S(1)}, u32[]{:S(2)}, u32[]{:S(2)}) %collective-permute-start.29) | collective-permute-done | bytes 131104 | tf_op jit(solution)/shard_map/ppermute | solution.py:399
  158.7 0.6 copy-done.23
  159.4 7.9 %sens.8 = bf16[256,4096]{1,0:T(8,128)(2,1)} custom-call(s32[6]{0:T(128)} %stack.27.pos, bf16[2048,8192]{1,0:T(8,128)(2,1)S(1)} %get-tuple-element.83.slab, bf16[256,256]{1,0:T(8,128)(2,1)} %get-tuple-element.134.refs_0_, bf16[256,256]{1,0:T(8,128)(2,1)} %copy-done.19, bf16[256,256]{1,0:T(8,128)(2,1)} %copy-done.18, bf16[256,256]{1,0:T(8,128)(2,1)} %copy-done.16, ...), custom_call_target="tpu_custom_call" | custom-call | flops 1717986944 | bytes 838860 | tf_op jit(solution)/shard_map/sens/pallas_call | solution.py:307
  168.8 1.5 collective-permute-done.35.came
  170.3 1.0 copy-done.6
  171.2 3.0 %pair_sum.7 = (f32[256,256]{1,0:T(8,128)}, bf16[256,256]{1,0:T(8,128)(2,1)}, bf16[256,256]{1,0:T(8,128)(2,1)}, bf16[256,256]{1,0:T(8,128)(2,1)}) custom-call(s32[6]{0:T(128)} %stack.27.pos, bf16[2048,8192]{1,0:T(8,128)(2,1)S(1)} %get-tuple-element.83.slab, f32[1024,256]{1,0:T(8,128)} %get-tuple-element.139.keep, f32[1024,256]{1,0:T(8,128)} %copy-done.6), custom_call_target="tpu_custom_call" | custom-call | flops 104857 | bytes 1048576 | tf_op jit(solution)/shard_map/pair_sum/pallas_call | solution.py:188
  174.3 8.5 %sens.9 = bf16[256,4096]{1,0:T(8,128)(2,1)} custom-call(s32[6]{0:T(128)} %stack.27.pos, bf16[2048,8192]{1,0:T(8,128)(2,1)S(1)} %get-tuple-element.83.slab, bf16[256,256]{1,0:T(8,128)(2,1)} %get-tuple-element.127.refs_0_, bf16[256,256]{1,0:T(8,128)(2,1)} %copy-done.11, bf16[256,256]{1,0:T(8,128)(2,1)} %copy-done.10, bf16[256,256]{1,0:T(8,128)(2,1)} %copy-done.9, ...), custom_call_target="tpu_custom_call" | custom-call | flops 1717986944 | bytes 838860 | tf_op jit(solution)/shard_map/sens/pallas_call | solution.py:307
  182.8 0.6 collective-permute-start.49
  183.4 8.4 %sens.10 = bf16[256,4096]{1,0:T(8,128)(2,1)} custom-call(s32[6]{0:T(128)} %stack.27.pos, bf16[2048,8192]{1,0:T(8,128)(2,1)S(1)} %get-tuple-element.83.slab, bf16[256,256]{1,0:T(8,128)(2,1)} %get-tuple-element.134.refs_0_, bf16[256,256]{1,0:T(8,128)(2,1)} %copy-done.19, bf16[256,256]{1,0:T(8,128)(2,1)} %copy-done.18, bf16[256,256]{1,0:T(8,128)(2,1)} %copy-done.16, ...), custom_call_target="tpu_custom_call" | custom-call | flops 1717986944 | bytes 838860 | tf_op jit(solution)/shard_map/sens/pallas_call | solution.py:307
  191.9 1.1 collective-permute-start.48
  192.9 0.8 collective-permute-start.38
  193.7 22.9 %collective-permute-done.36.refs_8_ = bf16[256,4096]{1,0:T(8,128)(2,1)} collective-permute-done((bf16[256,4096]{1,0:T(8,128)(2,1)}, bf16[256,4096]{1,0:T(8,128)(2,1)}, u32[]{:S(2)}, u32[]{:S(2)}) %collective-permute-start.36) | collective-permute-done | bytes 2097184 | tf_op jit(solution)/shard_map/ppermute | solution.py:393
  216.6 2.6 collective-permute-start.39
  219.7 5.6 %collective-permute-done.39.refs_1_ = bf16[256,256]{1,0:T(8,128)(2,1)S(1)} collective-permute-done((bf16[256,256]{1,0:T(8,128)(2,1)S(1)}, bf16[256,256]{1,0:T(8,128)(2,1)S(1)}, u32[]{:S(2)}, u32[]{:S(2)}) %collective-permute-start.39) | collective-permute-done | bytes 131104 | tf_op jit(solution)/shard_map/ppermute | solution.py:399
  225.4 0.6 copy-done.44
  226.1 3.0 %overload.7 = (f32[256,1024]{1,0:T(8,128)}, bf16[256,256]{1,0:T(8,128)(2,1)}) custom-call(s32[6]{0:T(128)} %stack.27.pos, bf16[2048,8192]{1,0:T(8,128)(2,1)S(1)} %get-tuple-element.83.slab, s32[16,128]{1,0:T(8,128)} %bitcast.10, f32[256,256]{1,0:T(8,128)} %get-tuple-element.147.mine, bf16[256,256]{1,0:T(8,128)(2,1)} %copy-done.38, ...), custom_call_target="tpu_custom_call", output_to_operand_aliasing={{0}: (7, {})} | custom-call | flops 524288 | bytes 419430 | tf_op jit(solution)/shard_map/overload/pallas_call | solution.py:245
  229.1 3.6 %collective-permute-start.43 = (bf16[256,256]{1,0:T(8,128)(2,1)}, bf16[256,256]{1,0:T(8,128)(2,1)S(1)}, u32[]{:S(2)}, u32[]{:S(2)}) collective-permute-start(bf16[256,256]{1,0:T(8,128)(2,1)} %get-tuple-element.154.refs_0_), channel_id=1, source_target_pairs={{0,6},{1,7},{2,0},{3,1},{4,2},{5,3},{6,4},{7,5},{8,14},{9,15},{10,... | collective-permute-start | bytes 393224 | tf_op jit(solution)/shard_map/ppermute | solution.py:399
  232.7 0.6 collective-permute-start.41
  233.3 2.7 collective-permute-done.43.refs_3_
  236.0 7.6 %collective-permute-done.42.refs_2_ = bf16[256,256]{1,0:T(8,128)(2,1)S(1)} collective-permute-done((bf16[256,256]{1,0:T(8,128)(2,1)}, bf16[256,256]{1,0:T(8,128)(2,1)S(1)}, u32[]{:S(2)}, u32[]{:S(2)}) %collective-permute-start.42) | collective-permute-done | bytes 131104 | tf_op jit(solution)/shard_map/ppermute | solution.py:399
  244.2 0.7 collective-permute-done.47.refs_7_
  245.7 0.6 copy-done.48
  246.4 13.6 %sens.11 = (f32[256,4096]{1,0:T(8,128)}, f32[256,4096]{1,0:T(8,128)}) custom-call(s32[6]{0:T(128)} %stack.27.pos, bf16[2048,8192]{1,0:T(8,128)(2,1)S(1)} %get-tuple-element.83.slab, bf16[256,256]{1,0:T(8,128)(2,1)} %get-tuple-element.154.refs_0_, bf16[256,256]{1,0:T(8,128)(2,1)} %copy-done.33, bf16[256,256]{1,0:T(8,128)(2,1)} %copy-done.32, ...), custom_call_target="tpu_custom_call" | custom-call | flops 3435973888 | bytes 1677721 | tf_op jit(solution)/shard_map/sens/pallas_call | solution.py:307
  260.6 2.2 copy-done
  262.8 3.2 %add_last.2.refs_0_ = f32[8192,256]{1,0:T(8,128)} custom-call(f32[256,4096]{1,0:T(8,128)S(1)} %copy-done, bf16[256,4096]{1,0:T(8,128)(2,1)S(1)} %collective-permute-done.49.came), custom_call_target="tpu_custom_call" | custom-call | flops 419430 | bytes 4194304 | tf_op jit(solution)/shard_map/add_last/pallas_call | solution.py:359
  266.1 3.2 %add_last.3 = f32[8192,256]{1,0:T(8,128)} custom-call(f32[256,4096]{1,0:T(8,128)S(1)} %copy-done.1, bf16[256,4096]{1,0:T(8,128)(2,1)S(1)} %collective-permute-done.48.came, f32[8192,256]{1,0:T(8,128)} %add_last.2.refs_0_), custom_call_target="tpu_custom_call", output_to_operand_aliasing={{}: (2, {})} | custom-call | flops 419430 | bytes 4194304 | tf_op jit(solution)/shard_map/add_last/pallas_call | solution.py:359
  (169 shorter events, 10.9 us)
Async XLA Ops:
  17.4 3.0 %collective-permute-start = (f32[1024,256]{1,0:T(8,128)}, f32[1024,256]{1,0:T(8,128)S(1)}, u32[]{:S(2)}, u32[]{:S(2)}) collective-permute-start(f32[1024,256]{1,0:T(8,128)} %get-tuple-element.85), channel_id=1, source_target_pairs={{0,1},{1,0},{2,3},{3,2},{4,5},{5,4},{6,7},{7,6},{8,9},{9,8},{10,11... | collective-permute-start | bytes 3145736 | tf_op jit(solution)/shard_map/ppermute | solution.py:396
  24.4 20.7 %collective-permute-start.3 = (bf16[256,256]{1,0:T(8,128)(2,1)}, bf16[256,256]{1,0:T(8,128)(2,1)S(1)}, u32[]{:S(2)}, u32[]{:S(2)}) collective-permute-start(bf16[256,256]{1,0:T(8,128)(2,1)} %get-tuple-element.86), channel_id=1, source_target_pairs={{0,6},{1,7},{2,0},{3,1},{4,2},{5,3},{6,4},{7,5},{8,14},{9,15},{10,... | collective-permute-start | bytes 393224 | tf_op jit(solution)/shard_map/ppermute | solution.py:399
  29.4 15.6 %collective-permute-start.1 = (bf16[256,256]{1,0:T(8,128)(2,1)}, bf16[256,256]{1,0:T(8,128)(2,1)S(1)}, u32[]{:S(2)}, u32[]{:S(2)}) collective-permute-start(bf16[256,256]{1,0:T(8,128)(2,1)} %get-tuple-element.91), channel_id=1, source_target_pairs={{0,2},{1,3},{2,4},{3,5},{4,6},{5,7},{6,0},{7,1},{8,10},{9,11},{10,... | collective-permute-start | bytes 393224 | tf_op jit(solution)/shard_map/ppermute | solution.py:399
  29.4 15.7 %collective-permute-start.2 = (bf16[256,256]{1,0:T(8,128)(2,1)}, bf16[256,256]{1,0:T(8,128)(2,1)S(1)}, u32[]{:S(2)}, u32[]{:S(2)}) collective-permute-start(bf16[256,256]{1,0:T(8,128)(2,1)} %get-tuple-element.92), channel_id=1, source_target_pairs={{0,4},{1,5},{2,6},{3,7},{4,0},{5,1},{6,2},{7,3},{8,12},{9,13},{10,... | collective-permute-start | bytes 393224 | tf_op jit(solution)/shard_map/ppermute | solution.py:399
  49.0 5.0 %collective-permute-start.4 = (f32[1024,256]{1,0:T(8,128)S(1)}, f32[1024,256]{1,0:T(8,128)S(1)}, u32[]{:S(2)}, u32[]{:S(2)}) collective-permute-start(f32[1024,256]{1,0:T(8,128)S(1)} %copy-done.51), channel_id=1, source_target_pairs={{0,1},{1,0},{2,3},{3,2},{4,5},{5,4},{6,7},{7,6},{8,9},{9,8},{10,11... | collective-permute-start | bytes 3145736 | tf_op jit(solution)/shard_map/ppermute | solution.py:396
  49.1 28.0 %collective-permute-start.10 = (bf16[256,256]{1,0:T(8,128)(2,1)}, bf16[256,256]{1,0:T(8,128)(2,1)S(1)}, u32[]{:S(2)}, u32[]{:S(2)}) collective-permute-start(bf16[256,256]{1,0:T(8,128)(2,1)} %get-tuple-element.104.refs_0_), channel_id=1, source_target_pairs={{0,6},{1,7},{2,0},{3,1},{4,2},{5,3},{6,4},{7,5},{8,14},{9,15},{10,... | collective-permute-start | bytes 393224 | tf_op jit(solution)/shard_map/ppermute | solution.py:399
  52.0 25.3 %collective-permute-start.9 = (bf16[256,256]{1,0:T(8,128)(2,1)}, bf16[256,256]{1,0:T(8,128)(2,1)S(1)}, u32[]{:S(2)}, u32[]{:S(2)}) collective-permute-start(bf16[256,256]{1,0:T(8,128)(2,1)} %get-tuple-element.104.refs_0_), channel_id=1, source_target_pairs={{0,4},{1,5},{2,6},{3,7},{4,0},{5,1},{6,2},{7,3},{8,12},{9,13},{10,... | collective-permute-start | bytes 393224 | tf_op jit(solution)/shard_map/ppermute | solution.py:399
  54.0 23.3 %collective-permute-start.8 = (bf16[256,256]{1,0:T(8,128)(2,1)}, bf16[256,256]{1,0:T(8,128)(2,1)S(1)}, u32[]{:S(2)}, u32[]{:S(2)}) collective-permute-start(bf16[256,256]{1,0:T(8,128)(2,1)} %get-tuple-element.104.refs_0_), channel_id=1, source_target_pairs={{0,2},{1,3},{2,4},{3,5},{4,6},{5,7},{6,0},{7,1},{8,10},{9,11},{10,... | collective-permute-start | bytes 393224 | tf_op jit(solution)/shard_map/ppermute | solution.py:399
  58.0 19.8 %collective-permute-start.5 = (bf16[256,256]{1,0:T(8,128)(2,1)}, bf16[256,256]{1,0:T(8,128)(2,1)S(1)}, u32[]{:S(2)}, u32[]{:S(2)}) collective-permute-start(bf16[256,256]{1,0:T(8,128)(2,1)} %get-tuple-element.101), channel_id=1, source_target_pairs={{0,2},{1,3},{2,4},{3,5},{4,6},{5,7},{6,0},{7,1},{8,10},{9,11},{10,... | collective-permute-start | bytes 393224 | tf_op jit(solution)/shard_map/ppermute | solution.py:399
  59.5 17.6 %copy-start.55 = (bf16[256,256]{1,0:T(8,128)(2,1)S(1)}, bf16[256,256]{1,0:T(8,128)(2,1)}, u32[]{:S(2)}) copy-start(bf16[256,256]{1,0:T(8,128)(2,1)} %get-tuple-element.97) | copy-start | bytes 393220
  59.5 17.7 %copy-start.24 = (bf16[256,256]{1,0:T(8,128)(2,1)S(1)}, bf16[256,256]{1,0:T(8,128)(2,1)}, u32[]{:S(2)}) copy-start(bf16[256,256]{1,0:T(8,128)(2,1)} %get-tuple-element.104.refs_0_) | copy-start | bytes 393220
  59.5 18.4 %collective-permute-start.6 = (bf16[256,256]{1,0:T(8,128)(2,1)}, bf16[256,256]{1,0:T(8,128)(2,1)S(1)}, u32[]{:S(2)}, u32[]{:S(2)}) collective-permute-start(bf16[256,256]{1,0:T(8,128)(2,1)} %get-tuple-element.102), channel_id=1, source_target_pairs={{0,4},{1,5},{2,6},{3,7},{4,0},{5,1},{6,2},{7,3},{8,12},{9,13},{10,... | collective-permute-start | bytes 393224 | tf_op jit(solution)/shard_map/ppermute | solution.py:399
  77.1 5.0 %collective-permute-start.7 = (bf16[256,256]{1,0:T(8,128)(2,1)S(1)}, bf16[256,256]{1,0:T(8,128)(2,1)S(1)}, u32[]{:S(2)}, u32[]{:S(2)}) collective-permute-start(bf16[256,256]{1,0:T(8,128)(2,1)S(1)} %copy-done.55), channel_id=1, source_target_pairs={{0,6},{1,7},{2,0},{3,1},{4,2},{5,3},{6,4},{7,5},{8,14},{9,15},{10,... | collective-permute-start | bytes 393224 | tf_op jit(solution)/shard_map/ppermute | solution.py:399
  77.3 4.8 %collective-permute-start.11 = (bf16[256,256]{1,0:T(8,128)(2,1)S(1)}, bf16[256,256]{1,0:T(8,128)(2,1)S(1)}, u32[]{:S(2)}, u32[]{:S(2)}) collective-permute-start(bf16[256,256]{1,0:T(8,128)(2,1)S(1)} %copy-done.24), channel_id=1, source_target_pairs={{0,1},{1,0},{2,3},{3,2},{4,5},{5,4},{6,7},{7,6},{8,9},{9,8},{10,11... | collective-permute-start | bytes 393224 | tf_op jit(solution)/shard_map/ppermute | solution.py:396
  77.4 4.8 %collective-permute-start.12 = (bf16[256,256]{1,0:T(8,128)(2,1)S(1)}, bf16[256,256]{1,0:T(8,128)(2,1)S(1)}, u32[]{:S(2)}, u32[]{:S(2)}) collective-permute-start(bf16[256,256]{1,0:T(8,128)(2,1)S(1)} %collective-permute-done.8.refs_1_), channel_id=1, source_target_pairs={{0,1},{1,0},{2,3},{3,2},{4,5},{5,4},{6,7},{7,6},{8,9},{9,8},{10,11... | collective-permute-start | bytes 393224 | tf_op jit(solution)/shard_map/ppermute | solution.py:396
  77.9 18.7 %copy-start.26 = (bf16[256,256]{1,0:T(8,128)(2,1)}, bf16[256,256]{1,0:T(8,128)(2,1)S(1)}, u32[]{:S(2)}) copy-start(bf16[256,256]{1,0:T(8,128)(2,1)S(1)} %collective-permute-done.5.refs_0_) | copy-start | bytes 393220
  77.9 4.3 %collective-permute-start.13 = (bf16[256,256]{1,0:T(8,128)(2,1)S(1)}, bf16[256,256]{1,0:T(8,128)(2,1)S(1)}, u32[]{:S(2)}, u32[]{:S(2)}) collective-permute-start(bf16[256,256]{1,0:T(8,128)(2,1)S(1)} %collective-permute-done.9.refs_2_), channel_id=1, source_target_pairs={{0,1},{1,0},{2,3},{3,2},{4,5},{5,4},{6,7},{7,6},{8,9},{9,8},{10,11... | collective-permute-start | bytes 393224 | tf_op jit(solution)/shard_map/ppermute | solution.py:396
  78.0 18.6 %copy-start.28 = (bf16[256,256]{1,0:T(8,128)(2,1)}, bf16[256,256]{1,0:T(8,128)(2,1)S(1)}, u32[]{:S(2)}) copy-start(bf16[256,256]{1,0:T(8,128)(2,1)S(1)} %collective-permute-done.6.refs_1_) | copy-start | bytes 393220
  78.0 4.2 %collective-permute-start.14 = (bf16[256,256]{1,0:T(8,128)(2,1)S(1)}, bf16[256,256]{1,0:T(8,128)(2,1)S(1)}, u32[]{:S(2)}, u32[]{:S(2)}) collective-permute-start(bf16[256,256]{1,0:T(8,128)(2,1)S(1)} %collective-permute-done.10.refs_3_), channel_id=1, source_target_pairs={{0,1},{1,0},{2,3},{3,2},{4,5},{5,4},{6,7},{7,6},{8,9},{9,8},{10,11... | collective-permute-start | bytes 393224 | tf_op jit(solution)/shard_map/ppermute | solution.py:396
  82.1 14.4 %copy-start.30 = (bf16[256,256]{1,0:T(8,128)(2,1)}, bf16[256,256]{1,0:T(8,128)(2,1)S(1)}, u32[]{:S(2)}) copy-start(bf16[256,256]{1,0:T(8,128)(2,1)S(1)} %collective-permute-done.7.refs_2_) | copy-start | bytes 393220
  96.6 60.0 %collective-permute-start.26 = (bf16[256,4096]{1,0:T(8,128)(2,1)}, bf16[256,4096]{1,0:T(8,128)(2,1)S(1)}, u32[]{:S(2)}, u32[]{:S(2)}) collective-permute-start(bf16[256,4096]{1,0:T(8,128)(2,1)} %get-tuple-element.132), channel_id=1, source_target_pairs={{0,8},{8,0},{16,24},{24,16},{1,9},{9,1},{17,25},{25,17},{2,10},{10... | collective-permute-start | bytes 6291464 | tf_op jit(solution)/shard_map/ppermute | solution.py:393
  98.2 58.9 %collective-permute-start.27 = (bf16[256,4096]{1,0:T(8,128)(2,1)}, bf16[256,4096]{1,0:T(8,128)(2,1)S(1)}, u32[]{:S(2)}, u32[]{:S(2)}) collective-permute-start(bf16[256,4096]{1,0:T(8,128)(2,1)} %get-tuple-element.108), channel_id=1, source_target_pairs={{0,16},{8,24},{16,0},{24,8},{1,17},{9,25},{17,1},{25,9},{2,18},{10... | collective-permute-start | bytes 6291464 | tf_op jit(solution)/shard_map/ppermute | solution.py:393
  102.7 2.9 %collective-permute-start.15 = (f32[1024,256]{1,0:T(8,128)}, f32[1024,256]{1,0:T(8,128)S(1)}, u32[]{:S(2)}, u32[]{:S(2)}) collective-permute-start(f32[1024,256]{1,0:T(8,128)} %get-tuple-element.115), channel_id=1, source_target_pairs={{0,1},{1,0},{2,3},{3,2},{4,5},{5,4},{6,7},{7,6},{8,9},{9,8},{10,11... | collective-permute-start | bytes 3145736 | tf_op jit(solution)/shard_map/ppermute | solution.py:396
  102.8 6.9 %collective-permute-start.18 = (bf16[256,256]{1,0:T(8,128)(2,1)}, bf16[256,256]{1,0:T(8,128)(2,1)S(1)}, u32[]{:S(2)}, u32[]{:S(2)}) collective-permute-start(bf16[256,256]{1,0:T(8,128)(2,1)} %get-tuple-element.127.refs_0_), channel_id=1, source_target_pairs={{0,6},{1,7},{2,0},{3,1},{4,2},{5,3},{6,4},{7,5},{8,14},{9,15},{10,... | collective-permute-start | bytes 393224 | tf_op jit(solution)/shard_map/ppermute | solution.py:399
  104.7 12.9 %collective-permute-start.17 = (bf16[256,256]{1,0:T(8,128)(2,1)}, bf16[256,256]{1,0:T(8,128)(2,1)S(1)}, u32[]{:S(2)}, u32[]{:S(2)}) collective-permute-start(bf16[256,256]{1,0:T(8,128)(2,1)} %get-tuple-element.127.refs_0_), channel_id=1, source_target_pairs={{0,4},{1,5},{2,6},{3,7},{4,0},{5,1},{6,2},{7,3},{8,12},{9,13},{10,... | collective-permute-start | bytes 393224 | tf_op jit(solution)/shard_map/ppermute | solution.py:399
  105.6 11.9 %collective-permute-start.16 = (bf16[256,256]{1,0:T(8,128)(2,1)}, bf16[256,256]{1,0:T(8,128)(2,1)S(1)}, u32[]{:S(2)}, u32[]{:S(2)}) collective-permute-start(bf16[256,256]{1,0:T(8,128)(2,1)} %get-tuple-element.127.refs_0_), channel_id=1, source_target_pairs={{0,2},{1,3},{2,4},{3,5},{4,6},{5,7},{6,0},{7,1},{8,10},{9,11},{10,... | collective-permute-start | bytes 393224 | tf_op jit(solution)/shard_map/ppermute | solution.py:399
  109.7 32.9 %copy-start.9 = (bf16[256,256]{1,0:T(8,128)(2,1)}, bf16[256,256]{1,0:T(8,128)(2,1)S(1)}, u32[]{:S(2)}) copy-start(bf16[256,256]{1,0:T(8,128)(2,1)S(1)} %collective-permute-done.18.refs_3_) | copy-start | bytes 393220
  109.7 27.6 %collective-permute-start.21 = (bf16[256,256]{1,0:T(8,128)(2,1)}, bf16[256,256]{1,0:T(8,128)(2,1)S(1)}, u32[]{:S(2)}, u32[]{:S(2)}) collective-permute-start(bf16[256,256]{1,0:T(8,128)(2,1)} %get-tuple-element.116), channel_id=1, source_target_pairs={{0,6},{1,7},{2,0},{3,1},{4,2},{5,3},{6,4},{7,5},{8,14},{9,15},{10,... | collective-permute-start | bytes 393224 | tf_op jit(solution)/shard_map/ppermute | solution.py:399
  117.6 24.1 %copy-start.10 = (bf16[256,256]{1,0:T(8,128)(2,1)}, bf16[256,256]{1,0:T(8,128)(2,1)S(1)}, u32[]{:S(2)}) copy-start(bf16[256,256]{1,0:T(8,128)(2,1)S(1)} %collective-permute-done.17.refs_2_) | copy-start | bytes 393220
  117.6 19.6 %collective-permute-start.19 = (bf16[256,256]{1,0:T(8,128)(2,1)}, bf16[256,256]{1,0:T(8,128)(2,1)S(1)}, u32[]{:S(2)}, u32[]{:S(2)}) collective-permute-start(bf16[256,256]{1,0:T(8,128)(2,1)} %get-tuple-element.122), channel_id=1, source_target_pairs={{0,2},{1,3},{2,4},{3,5},{4,6},{5,7},{6,0},{7,1},{8,10},{9,11},{10,... | collective-permute-start | bytes 393224 | tf_op jit(solution)/shard_map/ppermute | solution.py:399
  117.6 23.6 %copy-start.11 = (bf16[256,256]{1,0:T(8,128)(2,1)}, bf16[256,256]{1,0:T(8,128)(2,1)S(1)}, u32[]{:S(2)}) copy-start(bf16[256,256]{1,0:T(8,128)(2,1)S(1)} %collective-permute-done.16.refs_1_) | copy-start | bytes 393220
  117.6 19.6 %collective-permute-start.20 = (bf16[256,256]{1,0:T(8,128)(2,1)}, bf16[256,256]{1,0:T(8,128)(2,1)S(1)}, u32[]{:S(2)}, u32[]{:S(2)}) collective-permute-start(bf16[256,256]{1,0:T(8,128)(2,1)} %get-tuple-element.123), channel_id=1, source_target_pairs={{0,4},{1,5},{2,6},{3,7},{4,0},{5,1},{6,2},{7,3},{8,12},{9,13},{10,... | collective-permute-start | bytes 393224 | tf_op jit(solution)/shard_map/ppermute | solution.py:399
  141.1 14.8 %copy-start.12 = (bf16[256,256]{1,0:T(8,128)(2,1)S(1)}, bf16[256,256]{1,0:T(8,128)(2,1)}, u32[]{:S(2)}) copy-start(bf16[256,256]{1,0:T(8,128)(2,1)} %get-tuple-element.134.refs_0_) | copy-start | bytes 393220
  141.2 1.4 collective-permute-start.22
  141.2 1.5 collective-permute-start.23
  141.7 1.6 collective-permute-start.24
  142.6 1.3 collective-permute-start.25
  142.8 10.0 %collective-permute-start.30 = (bf16[256,256]{1,0:T(8,128)(2,1)}, bf16[256,256]{1,0:T(8,128)(2,1)S(1)}, u32[]{:S(2)}, u32[]{:S(2)}) collective-permute-start(bf16[256,256]{1,0:T(8,128)(2,1)} %get-tuple-element.134.refs_0_), channel_id=1, source_target_pairs={{0,6},{1,7},{2,0},{3,1},{4,2},{5,3},{6,4},{7,5},{8,14},{9,15},{10,... | collective-permute-start | bytes 393224 | tf_op jit(solution)/shard_map/ppermute | solution.py:399
  143.3 12.6 %collective-permute-start.29 = (bf16[256,256]{1,0:T(8,128)(2,1)}, bf16[256,256]{1,0:T(8,128)(2,1)S(1)}, u32[]{:S(2)}, u32[]{:S(2)}) collective-permute-start(bf16[256,256]{1,0:T(8,128)(2,1)} %get-tuple-element.134.refs_0_), channel_id=1, source_target_pairs={{0,4},{1,5},{2,6},{3,7},{4,0},{5,1},{6,2},{7,3},{8,12},{9,13},{10,... | collective-permute-start | bytes 393224 | tf_op jit(solution)/shard_map/ppermute | solution.py:399
  143.9 12.0 %collective-permute-start.28 = (bf16[256,256]{1,0:T(8,128)(2,1)}, bf16[256,256]{1,0:T(8,128)(2,1)S(1)}, u32[]{:S(2)}, u32[]{:S(2)}) collective-permute-start(bf16[256,256]{1,0:T(8,128)(2,1)} %get-tuple-element.134.refs_0_), channel_id=1, source_target_pairs={{0,2},{1,3},{2,4},{3,5},{4,6},{5,7},{6,0},{7,1},{8,10},{9,11},{10,... | collective-permute-start | bytes 393224 | tf_op jit(solution)/shard_map/ppermute | solution.py:399
  155.9 1.4 collective-permute-start.31
  156.0 1.5 collective-permute-start.32
  156.5 1.3 collective-permute-start.33
  156.6 10.7 %copy-start.2 = (bf16[256,4096]{1,0:T(8,128)(2,1)}, bf16[256,4096]{1,0:T(8,128)(2,1)S(1)}, u32[]{:S(2)}) copy-start(bf16[256,4096]{1,0:T(8,128)(2,1)S(1)} %collective-permute-done.26.refs_8_) | copy-start | bytes 6291460
  156.6 1.5 collective-permute-start.34
  157.0 10.2 %copy-start.3 = (bf16[256,4096]{1,0:T(8,128)(2,1)}, bf16[256,4096]{1,0:T(8,128)(2,1)S(1)}, u32[]{:S(2)}) copy-start(bf16[256,4096]{1,0:T(8,128)(2,1)S(1)} %collective-permute-done.27.refs_8_) | copy-start | bytes 6291460
  167.3 3.0 %collective-permute-start.35 = (f32[1024,256]{1,0:T(8,128)}, f32[1024,256]{1,0:T(8,128)S(1)}, u32[]{:S(2)}, u32[]{:S(2)}) collective-permute-start(f32[1024,256]{1,0:T(8,128)} %get-tuple-element.140), channel_id=1, source_target_pairs={{0,1},{1,0},{2,3},{3,2},{4,5},{5,4},{6,7},{7,6},{8,9},{9,8},{10,11... | collective-permute-start | bytes 3145736 | tf_op jit(solution)/shard_map/ppermute | solution.py:396
  167.8 48.8 %collective-permute-start.36 = (bf16[256,4096]{1,0:T(8,128)(2,1)}, bf16[256,4096]{1,0:T(8,128)(2,1)}, u32[]{:S(2)}, u32[]{:S(2)}) collective-permute-start(bf16[256,4096]{1,0:T(8,128)(2,1)} %sens.7), channel_id=1, source_target_pairs={{0,8},{8,0},{16,24},{24,16},{1,9},{9,1},{17,25},{25,17},{2,10},{10... | collective-permute-start | bytes 6291464 | tf_op jit(solution)/shard_map/ppermute | solution.py:393
  168.3 50.8 %collective-permute-start.37 = (bf16[256,4096]{1,0:T(8,128)(2,1)}, bf16[256,4096]{1,0:T(8,128)(2,1)}, u32[]{:S(2)}, u32[]{:S(2)}) collective-permute-start(bf16[256,4096]{1,0:T(8,128)(2,1)} %sens.8), channel_id=1, source_target_pairs={{0,16},{8,24},{16,0},{24,8},{1,17},{9,25},{17,1},{25,9},{2,18},{10... | collective-permute-start | bytes 6291464 | tf_op jit(solution)/shard_map/ppermute | solution.py:393
  182.8 10.1 %copy-start.54 = (bf16[256,256]{1,0:T(8,128)(2,1)S(1)}, bf16[256,256]{1,0:T(8,128)(2,1)}, u32[]{:S(2)}) copy-start(bf16[256,256]{1,0:T(8,128)(2,1)} %get-tuple-element.148) | copy-start | bytes 393220
  182.8 33.8 %copy-start.53 = (bf16[256,256]{1,0:T(8,128)(2,1)S(1)}, bf16[256,256]{1,0:T(8,128)(2,1)}, u32[]{:S(2)}) copy-start(bf16[256,256]{1,0:T(8,128)(2,1)} %get-tuple-element.149) | copy-start | bytes 393220
  182.8 36.4 %copy-start.52 = (bf16[256,256]{1,0:T(8,128)(2,1)S(1)}, bf16[256,256]{1,0:T(8,128)(2,1)}, u32[]{:S(2)}) copy-start(bf16[256,256]{1,0:T(8,128)(2,1)} %get-tuple-element.141) | copy-start | bytes 393220
  182.8 77.7 %collective-permute-start.49 = (bf16[256,4096]{1,0:T(8,128)(2,1)}, bf16[256,4096]{1,0:T(8,128)(2,1)S(1)}, u32[]{:S(2)}, u32[]{:S(2)}) collective-permute-start(bf16[256,4096]{1,0:T(8,128)(2,1)} %sens.9), channel_id=1, source_target_pairs={{0,8},{8,0},{16,24},{24,16},{1,9},{9,1},{17,25},{25,17},{2,10},{10... | collective-permute-start | bytes 6291464 | tf_op jit(solution)/shard_map/ppermute | solution.py:393
  191.9 74.1 %collective-permute-start.48 = (bf16[256,4096]{1,0:T(8,128)(2,1)}, bf16[256,4096]{1,0:T(8,128)(2,1)S(1)}, u32[]{:S(2)}, u32[]{:S(2)}) collective-permute-start(bf16[256,4096]{1,0:T(8,128)(2,1)} %sens.10), channel_id=1, source_target_pairs={{0,16},{8,24},{16,0},{24,8},{1,17},{9,25},{17,1},{25,9},{2,18},{10... | collective-permute-start | bytes 6291464 | tf_op jit(solution)/shard_map/ppermute | solution.py:393
  192.9 26.8 %collective-permute-start.38 = (bf16[256,256]{1,0:T(8,128)(2,1)S(1)}, bf16[256,256]{1,0:T(8,128)(2,1)S(1)}, u32[]{:S(2)}, u32[]{:S(2)}) collective-permute-start(bf16[256,256]{1,0:T(8,128)(2,1)S(1)} %copy-done.54), channel_id=1, source_target_pairs={{0,2},{1,3},{2,4},{3,5},{4,6},{5,7},{6,0},{7,1},{8,10},{9,11},{10,... | collective-permute-start | bytes 393224 | tf_op jit(solution)/shard_map/ppermute | solution.py:399
  216.6 8.8 %collective-permute-start.39 = (bf16[256,256]{1,0:T(8,128)(2,1)S(1)}, bf16[256,256]{1,0:T(8,128)(2,1)S(1)}, u32[]{:S(2)}, u32[]{:S(2)}) collective-permute-start(bf16[256,256]{1,0:T(8,128)(2,1)S(1)} %copy-done.53), channel_id=1, source_target_pairs={{0,4},{1,5},{2,6},{3,7},{4,0},{5,1},{6,2},{7,3},{8,12},{9,13},{10,... | collective-permute-start | bytes 393224 | tf_op jit(solution)/shard_map/ppermute | solution.py:399
  219.2 6.2 %collective-permute-start.40 = (bf16[256,256]{1,0:T(8,128)(2,1)S(1)}, bf16[256,256]{1,0:T(8,128)(2,1)S(1)}, u32[]{:S(2)}, u32[]{:S(2)}) collective-permute-start(bf16[256,256]{1,0:T(8,128)(2,1)S(1)} %copy-done.52), channel_id=1, source_target_pairs={{0,6},{1,7},{2,0},{3,1},{4,2},{5,3},{6,4},{7,5},{8,14},{9,15},{10,... | collective-permute-start | bytes 393224 | tf_op jit(solution)/shard_map/ppermute | solution.py:399
  229.1 6.9 %collective-permute-start.43 = (bf16[256,256]{1,0:T(8,128)(2,1)}, bf16[256,256]{1,0:T(8,128)(2,1)S(1)}, u32[]{:S(2)}, u32[]{:S(2)}) collective-permute-start(bf16[256,256]{1,0:T(8,128)(2,1)} %get-tuple-element.154.refs_0_), channel_id=1, source_target_pairs={{0,6},{1,7},{2,0},{3,1},{4,2},{5,3},{6,4},{7,5},{8,14},{9,15},{10,... | collective-permute-start | bytes 393224 | tf_op jit(solution)/shard_map/ppermute | solution.py:399
  232.7 10.9 %collective-permute-start.42 = (bf16[256,256]{1,0:T(8,128)(2,1)}, bf16[256,256]{1,0:T(8,128)(2,1)S(1)}, u32[]{:S(2)}, u32[]{:S(2)}) collective-permute-start(bf16[256,256]{1,0:T(8,128)(2,1)} %get-tuple-element.154.refs_0_), channel_id=1, source_target_pairs={{0,4},{1,5},{2,6},{3,7},{4,0},{5,1},{6,2},{7,3},{8,12},{9,13},{10,... | collective-permute-start | bytes 393224 | tf_op jit(solution)/shard_map/ppermute | solution.py:399
  232.7 10.9 %collective-permute-start.41 = (bf16[256,256]{1,0:T(8,128)(2,1)}, bf16[256,256]{1,0:T(8,128)(2,1)S(1)}, u32[]{:S(2)}, u32[]{:S(2)}) collective-permute-start(bf16[256,256]{1,0:T(8,128)(2,1)} %get-tuple-element.154.refs_0_), channel_id=1, source_target_pairs={{0,2},{1,3},{2,4},{3,5},{4,6},{5,7},{6,0},{7,1},{8,10},{9,11},{10,... | collective-permute-start | bytes 393224 | tf_op jit(solution)/shard_map/ppermute | solution.py:399
  236.0 8.1 %collective-permute-start.44 = (bf16[256,256]{1,0:T(8,128)(2,1)}, bf16[256,256]{1,0:T(8,128)(2,1)S(1)}, u32[]{:S(2)}, u32[]{:S(2)}) collective-permute-start(bf16[256,256]{1,0:T(8,128)(2,1)} %get-tuple-element.154.refs_0_), channel_id=1, source_target_pairs={{0,1},{1,0},{2,3},{3,2},{4,5},{5,4},{6,7},{7,6},{8,9},{9,8},{10,11... | collective-permute-start | bytes 393224 | tf_op jit(solution)/shard_map/ppermute | solution.py:396
  243.6 1.3 collective-permute-start.47
  243.6 1.5 collective-permute-start.46
  244.1 1.3 collective-permute-start.45
  (42 other events, 81.5 us)
